TPU v7x, 32 devices: a whole 2x2x4 slice. The times are simulated.
32 devices in a mesh: vars: 4 (over z), dp: 8 (over y, x, core).
Axes of the slice: x: 2, y: 2, z: 4, core: 2. Of those that a mesh axis runs over, the one named last changes fastest.
Arguments:
- fields: bfloat16 [72, 8, 4, 4, 1024], P('vars', 'dp'), may hold values from -6 to 6
- var_ids: int32 [72], P('vars'), may hold values from 0 to 71, each once
- segments: int32 [8, 4, 1024], P('dp', 'vars'), may hold values from 0 to 3, never falling along the last dimension, each value on 1 to 512 neighbouring positions
- condition: bfloat16 [8, 4, 384], P('dp', 'vars'), may hold values from -5 to 5
- cotangent: bfloat16 [8, 4, 1024, 384], P('dp', 'vars'), may hold values from -6 to 6
- slot_weights: float32 [72, 5, 384], P('vars'), may hold values from -3 to 3
- slot_momentum: float32 [72, 5, 384], P('vars'), may hold values from -2 to 2
- slot_average: float32 [72, 5, 384], P('vars'), may hold values from -3 to 3
- square: float32 [4, 384, 384], P(None, 'dp'), may hold values from -0.3125 to 0.3125
- square_momentum: float32 [4, 384, 384], P(None, 'dp'), may hold values from -4 to 4
- square_average: float32 [4, 384, 384], P(None, 'dp'), may hold values from -0.3125 to 0.3125
- wide: float32 [384, 3456], P('dp'), may hold values from -0.3125 to 0.3125
- wide_momentum: float32 [384, 3456], P('dp'), may hold values from -4 to 4
- wide_average: float32 [384, 3456], P('dp'), may hold values from -0.3125 to 0.3125
- mlp: float32 [2, 384, 1536], P(None, 'dp'), may hold values from -0.21875 to 0.21875
- mlp_momentum: float32 [2, 384, 1536], P(None, 'dp'), may hold values from -4 to 4
- mlp_average: float32 [2, 384, 1536], P(None, 'dp'), may hold values from -0.21875 to 0.21875
- vectors: float32 [11, 384], replicated, may hold values from -3 to 3
- vectors_momentum: float32 [11, 384], replicated, may hold values from -4 to 4
- vectors_average: float32 [11, 384], replicated, may hold values from -3 to 3
Outputs:
- block_out: bfloat16 [8, 4, 1024, 384], P('dp', 'vars')
- field_grad: float32 [72, 8, 4, 4, 1024], P('vars', 'dp')
- slot_grad: float32 [72, 5, 384], P('vars')
- slot_new: float32 [72, 5, 384], P('vars')
- slot_momentum_new: float32 [72, 5, 384], P('vars')
- slot_average_new: float32 [72, 5, 384], P('vars')
- square_grad: float32 [4, 384, 384], P(None, 'dp')
- square_new: float32 [4, 384, 384], P(None, 'dp')
- square_momentum_new: float32 [4, 384, 384], P(None, 'dp')
- square_average_new: float32 [4, 384, 384], P(None, 'dp')
- wide_grad: float32 [384, 3456], P('dp')
- wide_new: float32 [384, 3456], P('dp')
- wide_momentum_new: float32 [384, 3456], P('dp')
- wide_average_new: float32 [384, 3456], P('dp')
- mlp_grad: float32 [2, 384, 1536], P(None, 'dp')
- mlp_new: float32 [2, 384, 1536], P(None, 'dp')
- mlp_momentum_new: float32 [2, 384, 1536], P(None, 'dp')
- mlp_average_new: float32 [2, 384, 1536], P(None, 'dp')
- vectors_grad: float32 [11, 384], replicated
- vectors_new: float32 [11, 384], replicated
- vectors_momentum_new: float32 [11, 384], replicated
- vectors_average_new: float32 [11, 384], replicated
Inputs may be any that keep to these rules, and one draw needn't show every extreme that they name: Each number appears once; slot v holds variable var_ids[v] when that is below 69 and holds no variable otherwise. `segments`: ids never fall along a sequence; a segment has 1 to 512 patch slots, and one has exactly that many.
All inputs are finite; a program needn't handle non-finite values.
Results may differ from a plain program's by a relative error of at most 0.014.
Values may be sent and summed in bfloat16 or wider, within the bound.
A program may use at most 448 MiB of HBM per device.

v0:
```python
import functools
import math

import jax
import jax.numpy as jnp
from jax import lax
from jax.experimental import pallas as pl
from jax.experimental.pallas import tpu as pltpu
from jax.sharding import PartitionSpec as P

D = 384
HEADS = 6
HDIM = 64
PATCH = 4
NVARS = 69


NEGATIVE = -1e30
EPSILON = 1e-06
GELU_ROOT = math.sqrt(2.0 / math.pi)
GELU_CUBE = 0.044715
WIDTH = 128
VEC_ROWS = 16
MOMENTUM = 0.9
RATE = 0.05
EMBED_RATE = 0.5
AVERAGE_DECAY = 0.9
HIGHEST = lax.Precision.HIGHEST


def contract_cols(left, right):
    return lax.dot_general(
        left, right, (((1,), (1,)), ((), ())), preferred_element_type=jnp.float32
    )


def renew(weight, momentum, average, gradient, step_rate):
    new_momentum = MOMENTUM * momentum + gradient
    new_weight = weight - step_rate * (gradient + MOMENTUM * new_momentum)
    new_average = AVERAGE_DECAY * average + (1.0 - AVERAGE_DECAY) * new_weight
    return (gradient, new_weight, new_momentum, new_average)


TILE = 256
SLOT_ROWS = 80
AUGMENT = 80
FAR = -1e30


def matmul(left, right):
    return lax.dot_general(
        left, right, (((1,), (0,)), ((), ())), preferred_element_type=jnp.float32
    )


def halves(values):
    high = values.astype(jnp.bfloat16)
    return high, (values - high.astype(jnp.float32)).astype(jnp.bfloat16)


def fold(values):
    total = values[:, :WIDTH]
    for start in range(WIDTH, values.shape[1], WIDTH):
        total = total + values[:, start : start + WIDTH]
    return total


def block_kernel(
    tokens_all,
    groups,
    slots_each,
    ids_ref,
    fields_ref,
    slots_ref,
    mask_ref,
    square_ref,
    qkv_ref,
    mlp_ref,
    cols_ref,
    segment_ref,
    cot_ref,
    out_ref,
    grad_ref,
    slot_ref,
    vec_ref,
    field_ref,
    out_t,
    qkv_t,
    proj_t,
    up_t,
    down_t,
    slots_t,
    value_map,
    value_cols,
    score_map,
    probs,
    pooled,
    start,
    inverse,
    input_one,
    query,
    key,
    key_t,
    value,
    value_t,
    raw,
    mixed,
    log_sum,
    attended,
    input_two,
    active,
    grad_up,
    grad_branch,
    grad_mid,
    grad_att,
    grad_out,
    inner,
    grad_triple,
    map_acc,
    key_acc,
    column_acc,
    keyvec_ref,
    spans_ref,
):
    bfloat, flt = jnp.bfloat16, jnp.float32
    length = cot_ref.shape[0]
    tiles = length // TILE
    depth = D
    each = slots_each
    team_size = raw.shape[1]
    scale = HDIM ** (-0.5)

    def lanes(i):
        return pl.ds(pl.multiple_of(i * TILE, TILE), TILE)

    def column(which):
        return cols_ref[:, which : which + 1]

    out_t[...] = square_ref[2].astype(flt).T.astype(bfloat)
    proj_t[...] = square_ref[3].astype(flt).T.astype(bfloat)
    for block in range(3):
        part = slice(block * depth, (block + 1) * depth)
        qkv_t[part] = qkv_ref[:, part].astype(flt).T.astype(bfloat)
    for block in range(4):
        part = slice(block * depth, (block + 1) * depth)
        up_t[part] = mlp_ref[0, :, part].astype(flt).T.astype(bfloat)
        down_t[part] = mlp_ref[1, :, part].astype(flt).T.astype(bfloat)
    asked = cols_ref[:, 10:11]
    lane = lax.broadcasted_iota(jnp.int32, (depth, WIDTH), 1)
    head_of = lax.broadcasted_iota(jnp.int32, (depth, WIDTH), 0) // HDIM
    asked_high, asked_low = halves(jnp.where(lane == head_of, asked, 0.0))
    keyvec_ref[...] = (
        matmul(square_ref[0], asked_high) + matmul(square_ref[0], asked_low)
    ).astype(bfloat)
    firsts = [ids_ref[0, i * TILE] for i in range(tiles)]
    lasts = [ids_ref[0, (i + 1) * TILE - 1] for i in range(tiles)]
    for i in range(tiles):
        spans_ref[i, 0] = sum((lasts[j] < firsts[i]).astype(jnp.int32) for j in range(tiles))
        spans_ref[i, 1] = sum((firsts[j] <= lasts[i]).astype(jnp.int32) for j in range(tiles))
    slots = slots_ref[...]
    slots_high, slots_low = halves(slots)
    value_weight = square_ref[1]
    value_rows = matmul(slots_high, value_weight) + matmul(slots_low, value_weight)
    score_map[...] = matmul(slots_high, keyvec_ref[...]) + matmul(slots_low, keyvec_ref[...])
    turned_high, turned_low = halves(slots.T)
    slots_t[0] = turned_high
    slots_t[1] = turned_low
    value_turned = value_rows.T
    rows_high, rows_low = halves(value_turned)
    for head in range(HEADS):
        part = slice(head * HDIM, (head + 1) * HDIM)
        value_map[head, :HDIM] = rows_high[part]
        value_map[head, HDIM:] = rows_low[part]
        both = jnp.concatenate([value_turned[part], value_turned[part]], axis=0).T
        high = both.astype(bfloat)
        low = (both - high.astype(flt)).astype(bfloat)
        lane = lax.broadcasted_iota(jnp.int32, both.shape, 1)
        value_cols[head] = jnp.where(lane < HDIM, high.astype(flt), low.astype(flt)).astype(bfloat)
    column_acc[...] = jnp.zeros_like(column_acc)
    map_acc[...] = jnp.zeros_like(map_acc)
    key_acc[...] = jnp.zeros_like(key_acc)
    grad_triple[...] = jnp.zeros_like(grad_triple)

    def fields_at(i):
        return [fields_ref[p, :, lanes(i)].astype(flt) for p in range(PATCH)]

    def score_col(p, head):
        return score_map[p * SLOT_ROWS : (p + 1) * SLOT_ROWS, head : head + 1]

    def mixture(prob, fields):
        return jnp.concatenate([prob * f for f in fields] + [prob], axis=0).astype(bfloat)

    def normalize_cols(values):
        center = values - jnp.mean(values, axis=0, keepdims=True)
        inv = lax.rsqrt(jnp.mean(center * center, axis=0, keepdims=True) + EPSILON)
        return center * inv, inv

    def normalize_cols_back(grad, normed, inv):
        first = jnp.mean(grad, axis=0, keepdims=True)
        second = jnp.mean(grad * normed, axis=0, keepdims=True)
        return inv * (grad - first - normed * second)

    @pl.loop(0, tiles)
    def _(i):
        at = lanes(i)
        fields = fields_at(i)
        for head in range(HEADS):
            score = score_col(PATCH, head) + mask_ref[:, 0:1]
            for p in range(PATCH):
                score = score + score_col(p, head) * fields[p]
            score = score * scale
            weight = jnp.exp(score - jnp.max(score, axis=0, keepdims=True))
            prob = weight / jnp.sum(weight, axis=0, keepdims=True)
            probs[head, :, at] = prob
            both = matmul(value_map[head], mixture(prob, fields))
            part = slice(head * HDIM, (head + 1) * HDIM)
            total = both[:HDIM] + both[HDIM:] + cols_ref[part, 0:1]
            pooled[part, at] = total.astype(bfloat)
        begin = matmul(out_t[...], pooled[:, at]) + column(1)
        start[:, at] = begin
        normed, inv = normalize_cols(begin)
        inverse[0:1, at] = inv
        low = (normed * (1.0 + column(5)) + column(4)).astype(bfloat)
        input_one[:, at] = low
        segment = segment_ref[:, at]
        ident = lax.broadcasted_iota(jnp.int32, (AUGMENT - HDIM, TILE), 0)
        hot = jnp.where(ident == segment, 1.0, 0.0)
        cold = jnp.where((ident != segment) & (ident < 4), FAR, 0.0)
        for head in range(HEADS):
            part = slice(head * HDIM, (head + 1) * HDIM)
            queries = matmul(qkv_t[part], low).astype(bfloat).astype(flt) * scale
            query[head, :, at] = jnp.concatenate([queries, hot], axis=0).astype(bfloat)
            part = slice(depth + head * HDIM, depth + (head + 1) * HDIM)
            keys = matmul(qkv_t[part], low).astype(bfloat)
            key_t[head * HDIM : (head + 1) * HDIM, at] = keys
            long = jnp.concatenate([keys.astype(flt), cold], axis=0)
            key[head, at] = long.T.astype(bfloat)
            part = slice(2 * depth + head * HDIM, 2 * depth + (head + 1) * HDIM)
            values = matmul(qkv_t[part], low).astype(bfloat)
            value[head, at] = values.astype(flt).T.astype(bfloat)
            value_t[head, :HDIM, at] = values
            value_t[head, HDIM:, at] = jnp.ones((AUGMENT - HDIM, TILE), bfloat)

    @pl.loop(0, tiles)
    def _(i):
        at = lanes(i)
        low, high = spans_ref[i, 0], spans_ref[i, 1]

        mixed[...] = jnp.zeros_like(mixed)
        for base in range(0, HEADS, team_size):
            team = range(base, base + team_size)

            def scores(j, tops, team=team, base=base):
                new = []
                for head in team:
                    logits = matmul(key[head, lanes(j)], query[head, :, at])
                    raw[j, head - base] = logits
                    top = jnp.max(logits, axis=0, keepdims=True)
                    new.append(jnp.maximum(tops[head - base], top))
                return tuple(new)

            none = tuple(jnp.full((1, TILE), FAR, flt) for _ in team)
            tops = lax.fori_loop(low, high, scores, none)

            def blend(j, totals, team=team, base=base, tops=tops):
                new = []
                for head in team:
                    weight = jnp.exp(raw[j, head - base] - tops[head - base])
                    new.append(totals[head - base] + jnp.sum(weight, axis=0, keepdims=True))
                    mixed[head] += matmul(value_t[head, :, lanes(j)], weight.astype(bfloat))
                return tuple(new)

            zero = tuple(jnp.zeros((1, TILE), flt) for _ in team)
            totals = lax.fori_loop(low, high, blend, zero)
            for head in team:
                part = slice(head * HDIM, (head + 1) * HDIM)
                whole = mixed[head, :HDIM] / mixed[head, HDIM : HDIM + 1]
                upper, rest = halves(whole)
                attended[part, at] = upper
                grad_out[part, at] = rest
                log_sum[head : head + 1, at] = tops[head - base] + jnp.log(totals[head - base])

    rate = 1.0 / math.sqrt(tokens_all)

    @pl.loop(0, tiles)
    def _(i):
        at = lanes(i)
        att = attended[:, at]
        att_branch = matmul(proj_t[...], att) + column(2)
        mid = start[:, at] + column(6) * att_branch
        normed, inv = normalize_cols(mid)
        low = (normed * (1.0 + column(8)) + column(7)).astype(bfloat)
        input_two[:, at] = low
        out = column(3) + jnp.zeros((depth, TILE), flt)
        for block in range(HEADS):
            part = slice(block * TILE, (block + 1) * TILE)
            up = matmul(up_t[part], low)
            square = up * up
            curve = jnp.tanh(up * (GELU_ROOT + (GELU_ROOT * GELU_CUBE) * square))
            half = 0.5 + 0.5 * curve
            act = (up * half).astype(bfloat)
            active[part, at] = act
            slope = half + (0.5 * up) * (1.0 - curve * curve) * (
                GELU_ROOT + (3.0 * GELU_ROOT * GELU_CUBE) * square
            )
            raw[block // team_size, block % team_size] = slope
            out = out + matmul(mlp_ref[1, :, part], act)
        result = mid + column(9) * out
        rows = pl.ds(pl.multiple_of(i * TILE, TILE), TILE)
        out_ref[rows] = result.T.astype(bfloat)
        grad = cot_ref[rows].astype(flt).T * rate
        column_acc[9] += fold(grad * out)
        low_grad = (grad * column(9)).astype(bfloat)
        grad_branch[:, at] = low_grad
        column_acc[3] += fold(low_grad.astype(flt))
        grad_in = jnp.zeros((depth, TILE), flt)
        for block in range(HEADS):
            part = slice(block * TILE, (block + 1) * TILE)
            ups = (matmul(down_t[part], low_grad) * raw[block // team_size, block % team_size]).astype(bfloat)
            grad_up[part, at] = ups
            grad_in = grad_in + matmul(mlp_ref[0, :, part], ups)
        column_acc[8] += fold(grad_in * normed)
        column_acc[7] += fold(grad_in)
        grad = grad + normalize_cols_back(grad_in * (1.0 + column(8)), normed, inv)
        grad_mid[:, at] = grad
        column_acc[6] += fold(grad * att_branch)
        low_grad = (grad * column(6)).astype(bfloat)
        grad_att[:, at] = low_grad
        column_acc[2] += fold(low_grad.astype(flt))
        grads = matmul(square_ref[3], low_grad)
        low_grad = grads.astype(bfloat)
        whole = att.astype(flt) + grad_out[:, at].astype(flt)
        product = low_grad.astype(flt) * whole
        grad_out[:, at] = low_grad
        for head in range(HEADS):
            part = slice(head * HDIM, (head + 1) * HDIM)
            inner[head : head + 1, at] = jnp.sum(product[part], axis=0, keepdims=True)

    def weight_grad(left, right, rows, base):
        for block in range(0, rows, TILE):
            size = min(TILE, rows - block)
            grads = contract_cols(left[...], right[block : block + size])
            for piece in range(size // WIDTH):
                place = base + block // WIDTH + piece
                grad_ref[place] = grads[:, piece * WIDTH : (piece + 1) * WIDTH].astype(bfloat)

    weight_grad(input_two, grad_up, 4 * depth, 0)
    weight_grad(grad_branch, active, 4 * depth, 12)
    weight_grad(attended, grad_att, depth, 33)

    @pl.loop(0, tiles)
    def _(i):
        at = lanes(i)

        @pl.loop(spans_ref[i, 0], spans_ref[i, 1])
        def _(j):
            to = lanes(j)
            for head in range(HEADS):
                part = slice(head * HDIM, (head + 1) * HDIM)
                queries = query[head, :, at]
                logits = matmul(key[head, to], queries)
                prob = jnp.exp(logits - log_sum[head : head + 1, at])
                grads = grad_out[part, at]
                back = matmul(value[head, to], grads)
                grad_raw = (prob * (back - inner[head : head + 1, at])).astype(bfloat)
                grad_triple[part, at] += matmul(key_t[part, to], grad_raw)
                part = slice(depth + head * HDIM, depth + (head + 1) * HDIM)
                grad_triple[part, to] += contract_cols(queries[:HDIM], grad_raw)
                part = slice(2 * depth + head * HDIM, 2 * depth + (head + 1) * HDIM)
                grad_triple[part, to] += contract_cols(grads, prob.astype(bfloat))

    @pl.loop(0, tiles)
    def _(i):
        at = lanes(i)
        grad_in = jnp.zeros((depth, TILE), flt)
        for block in range(3):
            part = slice(block * depth, (block + 1) * depth)
            grads = grad_triple[part, at]
            if block == 0:
                grads = grads * scale
            grads = grads.astype(bfloat)
            active[part, at] = grads
            grad_in = grad_in + matmul(qkv_ref[:, part], grads)
        inv = inverse[0:1, at]
        begin = start[:, at]
        normed = (begin - jnp.mean(begin, axis=0, keepdims=True)) * inv
        column_acc[5] += fold(grad_in * normed)
        column_acc[4] += fold(grad_in)
        grad = grad_mid[:, at] + normalize_cols_back(grad_in * (1.0 + column(5)), normed, inv)
        low_grad = grad.astype(bfloat)
        attended[:, at] = low_grad
        column_acc[1] += fold(low_grad.astype(flt))
        grads = matmul(square_ref[2], low_grad).astype(bfloat)
        column_acc[0] += fold(grads.astype(flt))
        fields = fields_at(i)
        field_grads = [jnp.zeros((SLOT_ROWS, TILE), flt) for _ in range(PATCH)]
        for head in range(HEADS):
            part = slice(head * HDIM, (head + 1) * HDIM)
            own = grads[part]
            prob = probs[head, :, at]
            cross = matmul(value_cols[head], jnp.concatenate([own, own], axis=0))
            pieces = [cross[p * SLOT_ROWS : (p + 1) * SLOT_ROWS] for p in range(PATCH + 1)]
            along = pieces[PATCH]
            for p in range(PATCH):
                along = along + pieces[p] * fields[p]
            center = jnp.sum(prob * along, axis=0, keepdims=True)
            grad_score = (prob * (along - center) * scale).astype(bfloat).astype(flt)
            for p in range(PATCH):
                field_grads[p] = (
                    field_grads[p] + prob * pieces[p] + grad_score * score_col(p, head)
                )
                key_acc[head, p] += fold(fields[p] * grad_score)
            key_acc[head, PATCH] += fold(grad_score)
            map_acc[part] += contract_cols(own, mixture(prob, fields))
        for group in range(groups):
            pieces = [grad[group * each : (group + 1) * each] for grad in field_grads]
            pieces.append(jnp.zeros((field_ref.shape[1] - PATCH * each, TILE), flt))
            field_ref[group, :, at] = jnp.concatenate(pieces, axis=0).astype(bfloat)

    weight_grad(input_one, active, 3 * depth, 24)
    weight_grad(pooled, attended, depth, 36)
    maps_high, maps_low = halves(map_acc[...])
    value_grad = (
        contract_cols(slots_t[0], maps_high)
        + contract_cols(slots_t[0], maps_low)
        + contract_cols(slots_t[1], maps_high)
    )
    for piece in range(3):
        part = slice(piece * WIDTH, (piece + 1) * WIDTH)
        grad_ref[39 + piece] = value_grad[:, part].astype(bfloat)
    lane = lax.broadcasted_iota(jnp.int32, (SLOT_ROWS, WIDTH), 1)
    keys = []
    for p in range(PATCH + 1):
        rows = jnp.zeros((SLOT_ROWS, WIDTH), flt)
        for head in range(HEADS):
            rows = rows + jnp.where(
                lane == head, jnp.sum(key_acc[head, p], axis=1, keepdims=True), 0.0
            )
        keys.append(rows)
    keys = jnp.concatenate(keys, axis=0)
    keys_high, keys_low = halves(keys)
    key_grad = (
        matmul(slots_t[0], keys_high) + matmul(slots_t[0], keys_low) + matmul(slots_t[1], keys_high)
    )
    grad_ref[42] = key_grad.astype(bfloat)
    grad_ref[43] = jnp.zeros_like(grad_ref[43])
    slot_grad = (
        matmul(value_weight, maps_high)
        + matmul(value_weight, maps_low)
        + contract_cols(keyvec_ref[...], keys_high)
        + contract_cols(keyvec_ref[...], keys_low)
    )
    turned = slot_grad.T
    pairs, rows = slot_ref.shape[1], slot_ref.shape[3]
    size = slot_share((PATCH + 1) * each, 2 * pairs)
    for group in range(groups):
        pieces = [
            turned[p * SLOT_ROWS + group * each : p * SLOT_ROWS + (group + 1) * each][
                :, piece * WIDTH : (piece + 1) * WIDTH
            ]
            for piece in range(3)
            for p in range(PATCH + 1)
        ]
        used = 3 * (PATCH + 1) * each
        pieces.append(jnp.zeros((2 * pairs * size + rows - used, WIDTH), flt))
        flat = jnp.concatenate(pieces, axis=0)
        for block in range(2 * pairs):
            part = flat[block * size : block * size + rows]
            slot_ref[group, block // 2, block % 2] = part.astype(bfloat)
    grad_high, grad_low = halves(key_grad)
    key_turned = square_ref[0].astype(flt).T.astype(bfloat)
    asked = matmul(key_turned, grad_high) + matmul(key_turned, grad_low)
    lane = lax.broadcasted_iota(jnp.int32, (depth, WIDTH), 1)
    head_of = lax.broadcasted_iota(jnp.int32, (depth, WIDTH), 0) // HDIM
    columns = jnp.where(
        lane == 0, jnp.sum(jnp.where(lane == head_of, asked, 0.0), axis=1, keepdims=True), 0.0
    )
    columns = columns + jnp.where(lane == 11, cols_ref[:, 11:12], 0.0)
    for which in range(10):
        columns = columns + jnp.where(
            lane == which + 1, jnp.sum(column_acc[which], axis=1, keepdims=True), 0.0
        )
    vec_ref[...] = columns.T[:VEC_ROWS]


def slot_share(rows, count):
    return -(-3 * rows // count)


def block_step(count, groups, own, each, segment, fields, slots, mask, square, qkv, mlp, cols, cot):
    length = cot.shape[0]
    bfloat, flt = jnp.bfloat16, jnp.float32
    rows = (PATCH + 1) * SLOT_ROWS
    tiles = length // TILE
    block_rows = -(-own // 16) * 16
    field_rows = -(-PATCH * each // 16) * 16
    team_size = HEADS if count * block_rows <= D else HEADS // 2
    vmem = pl.BlockSpec(memory_space=pltpu.VMEM)
    shapes = [
        ((D, D), bfloat),
        ((3 * D, D), bfloat),
        ((D, D), bfloat),
        ((4 * D, D), bfloat),
        ((4 * D, D), bfloat),
        ((2, D, rows), bfloat),
        ((HEADS, 2 * HDIM, rows), bfloat),
        ((HEADS, rows, 2 * HDIM), bfloat),
        ((rows, WIDTH), flt),
        ((HEADS, SLOT_ROWS, length), flt),
        ((D, length), bfloat),
        ((D, length), flt),
        ((8, length), flt),
        ((D, length), bfloat),
        ((HEADS, AUGMENT, length), bfloat),
        ((HEADS, length, AUGMENT), bfloat),
        ((D, length), bfloat),
        ((HEADS, length, HDIM), bfloat),
        ((HEADS, AUGMENT, length), bfloat),
        ((tiles, team_size, TILE, TILE), flt),
        ((HEADS, AUGMENT, TILE), flt),
        ((8, length), flt),
        ((D, length), bfloat),
        ((D, length), bfloat),
        ((4 * D, length), bfloat),
        ((4 * D, length), bfloat),
        ((D, length), bfloat),
        ((D, length), flt),
        ((D, length), bfloat),
        ((D, length), bfloat),
        ((8, length), flt),
        ((3 * D, length), flt),
        ((D, rows), flt),
        ((HEADS, PATCH + 1, SLOT_ROWS, WIDTH), flt),
        ((10, D, WIDTH), flt),
        ((D, WIDTH), bfloat),
    ]
    return pl.pallas_call(
        functools.partial(block_kernel, groups * count * length, groups, each),
        out_shape=(
            jax.ShapeDtypeStruct((length, D), bfloat),
            jax.ShapeDtypeStruct((44, D, WIDTH), bfloat),
            jax.ShapeDtypeStruct((groups, count // 2, 2, block_rows, WIDTH), bfloat),
            jax.ShapeDtypeStruct((VEC_ROWS, D), flt),
            jax.ShapeDtypeStruct((groups, field_rows, length), bfloat),
        ),
        in_specs=[pl.BlockSpec(memory_space=pltpu.SMEM)] + [vmem] * 9,
        out_specs=(vmem,) * 5,
        scratch_shapes=[pltpu.VMEM(shape, dtype) for shape, dtype in shapes]
        + [pltpu.SMEM((tiles, 2), jnp.int32)],
        compiler_params=pltpu.CompilerParams(vmem_limit_bytes=62 << 20),
    )(segment, fields, slots, mask, square, qkv, mlp, cols, segment, cot)


CHUNKS = 4
CHUNK = 12
ORDER = (3, 0, 1, 2)
WIDTH = 128
VEC_ROWS = 16
MESH = pl.DeviceIdType.MESH


def flip(index, mask, bits):
    total = 0
    for bit in range(bits):
        own = (index // 2**bit) % 2
        total = total + (1 - own if (mask >> bit) & 1 else own) * 2**bit
    return total


def rounds_of(bits, backward):
    order = list(range(bits))
    return order[::-1] if backward else order


def mask_of(order, level, entry):
    mask = 0
    for place, bit in enumerate(order[level:]):
        if (entry >> (len(order) - level - 1 - place)) & 1:
            mask |= 1 << bit
    return mask


def greet(dp, here, masks, bits, groups):
    barrier = pltpu.get_barrier_semaphore()
    for mask in masks:
        pl.semaphore_signal(
            barrier, inc=1, device_id={"dp": flip(dp, mask, bits)}, device_id_type=MESH
        )
    for step in range(1, groups):
        pl.semaphore_signal(
            barrier, inc=1, device_id={"vars": (here + step) % groups}, device_id_type=MESH
        )
    pl.semaphore_wait(barrier, len(masks) + groups - 1)


class Copies:
    def __init__(self, send_sem, recv_sem):
        self.send_sem, self.recv_sem = send_sem, recv_sem
        self.started = []

    def start(self, source, target, device):
        place = len(self.started)
        copy = pltpu.make_async_remote_copy(
            src_ref=source,
            dst_ref=target,
            send_sem=self.send_sem.at[place],
            recv_sem=self.recv_sem.at[place],
            device_id=device,
            device_id_type=MESH,
        )
        copy.start()
        self.started.append(copy)
        return copy

    def finish(self):
        for copy in self.started:
            copy.wait_send()


class Spread:
    def __init__(self, copies, refs, dp, bits, order):
        self.copies, self.refs, self.dp, self.bits = copies, refs, dp, bits
        self.order = order
        self.arriving = {}

    def send(self, mask, first):
        block = flip(self.dp, mask, self.bits)
        for level in range(first, len(self.order)):
            bit = self.order[level]
            partner = {"dp": flip(self.dp, 1 << bit, self.bits)}
            for ref in self.refs:
                copy = self.copies.start(ref(block), ref(block), partner)
                self.arriving.setdefault(level, []).append((mask | (1 << bit), copy))

    def begin(self):
        self.send(0, 0)

    def advance(self, level):
        for place, (mask, copy) in enumerate(self.arriving[level]):
            copy.wait_recv()
            if place % len(self.refs) == len(self.refs) - 1:
                self.send(mask, level + 1)


def reduce_kernel(
    count,
    groups,
    g_ref,
    s_ref,
    vec_ref,
    field_ref,
    total,
    slot_ref,
    vec_all,
    field_out,
    recv0,
    acc,
    send_x,
    recv_x,
    zsend,
    zrecv,
    zkeep,
    ysend,
    yrecv,
    send_sem,
    recv_sem,
):
    bits = count.bit_length() - 1
    lower = bits - 1
    dp, here = lax.axis_index("dp"), lax.axis_index("vars")
    core, pair = dp % 2, dp // 2
    greet(dp, here, [1 << bit for bit in range(bits)], bits, groups)
    copies = Copies(send_sem, recv_sem)
    half = CHUNK // 2
    share = CHUNK // groups
    other = {"dp": dp + 1 - 2 * core}

    def grads_at(piece):
        if piece < 2 * CHUNKS - 2:
            return piece * half, half
        size = half - groups // 2
        return (2 * CHUNKS - 2) * half + (piece % 2) * size, size

    vec_copies = [
        copies.start(vec_ref, vec_all.at[dp, here], {"vars": (here + step) % groups})
        for step in range(1, groups)
    ]
    vec_all[dp, here] = vec_ref[...]
    level0 = {}
    for chunk in ORDER:
        for side in range(2):
            piece = 2 * chunk + side
            base, size = grads_at(piece)
            level0[piece] = [
                copies.start(
                    g_ref.at[pl.ds(base, size), :, 1 - core],
                    recv0.at[piece, pl.ds(0, size)],
                    other,
                )
            ]
            if size < half:
                level0[piece].append(
                    copies.start(
                        s_ref.at[pl.ds(side * (half - size), half - size), :, 1 - core],
                        recv0.at[piece, pl.ds(size, half - size)],
                        other,
                    )
                )
    field_copies = [
        copies.start(
            field_ref.at[(here + step) % groups],
            field_out.at[here],
            {"vars": (here + step) % groups},
        )
        for step in range(1, groups)
    ]
    field_out[here] = field_ref[here]
    forth = list(range(1, bits)) + [0]
    vecs = Spread(copies, [lambda block: vec_all.at[block]], dp, bits, forth)
    slots = Spread(copies, [lambda block: slot_ref.at[block]], dp, bits, forth)

    def vec_begin():
        for copy in vec_copies:
            copy.wait_recv()
        vecs.begin()

    crossing = {}

    def send_level(piece, level):
        order = rounds_of(lower, piece % 2)
        entries = 2 ** (lower - 1 - level)
        low = 2**lower - 2 ** (lower - level)
        partner = {"dp": 2 * flip(pair, 1 << order[level], lower) + core}
        crossing[piece, level] = copies.start(
            send_x.at[piece, pl.ds(low, entries)],
            recv_x.at[piece, pl.ds(low, entries)],
            partner,
        )

    def first(piece):
        order = rounds_of(lower, piece % 2)
        for copy in level0[piece]:
            copy.wait_recv()
        base, size = grads_at(piece)
        kept = 2 ** (lower - 1)
        for entry in range(2**lower):
            block = flip(pair, mask_of(order, 0, entry), lower)
            value = g_ref[pl.ds(base, size), block, core].astype(jnp.float32)
            value = value + recv0[piece, pl.ds(0, size), block].astype(jnp.float32)
            if size < half:
                rest = half - size
                slots = s_ref[pl.ds((piece % 2) * rest, rest), block, core].astype(jnp.float32)
                slots = slots + recv0[piece, pl.ds(size, rest), block].astype(jnp.float32)
                value = jnp.concatenate([value[:2], slots[:1], value[2:], slots[1:]], axis=0)
            if entry < kept:
                acc[piece, entry] = value
            else:
                send_x[piece, entry - kept] = value.astype(jnp.bfloat16)
        send_level(piece, 0)

    def later(piece, level):
        crossing[piece, level].wait_recv()
        entries = 2 ** (lower - 1 - level)
        low = 2**lower - 2 ** (lower - level)
        kept = entries // 2
        for entry in range(entries):
            value = acc[piece, entry] + recv_x[piece, low + entry].astype(jnp.float32)
            if entries > 1 and entry >= kept:
                send_x[piece, low + entries + entry - kept] = value.astype(jnp.bfloat16)
            else:
                acc[piece, entry] = value
        if level + 1 < lower:
            send_level(piece, level + 1)

    near = {"vars": here + 1 - 2 * (here % 2)}
    far = {"vars": (here + 2) % groups}
    low, top = here % 2, here // 2
    across, over, around, forward = {}, {}, {}, {}

    def send_near(piece):
        zsend[piece] = acc[piece, 0, pl.ds(share * (1 - low), share)].astype(jnp.bfloat16)
        across[piece] = copies.start(zsend.at[piece], zrecv.at[piece], near)

    def sum_near(piece):
        across[piece].wait_recv()
        own = acc[piece, 0, pl.ds(share * low, share)]
        zkeep[piece] = own + zrecv[piece].astype(jnp.float32)

    def send_far(chunk):
        for side in range(2):
            sum_near(2 * chunk + side)
        ysend[chunk] = zkeep[2 * chunk + 1 - top].astype(jnp.bfloat16)
        over[chunk] = copies.start(ysend.at[chunk], yrecv.at[chunk], far)

    def quarter(chunk, which):
        count_back = share - 1 if chunk == CHUNKS - 1 else share
        return total.at[chunk, which, pl.ds(0, count_back)]

    def sum_far(chunk):
        over[chunk].wait_recv()
        value = zkeep[2 * chunk + top] + yrecv[chunk].astype(jnp.float32)
        total[chunk, here] = value.astype(jnp.bfloat16)
        if chunk == CHUNKS - 1:
            slot_ref[dp] = value[share - 1]
        around[chunk] = [
            copies.start(quarter(chunk, here), quarter(chunk, here), to) for to in (far, near)
        ]

    def pass_on(chunk):
        around[chunk][0].wait_recv()
        other_quarter = quarter(chunk, (here + 2) % groups)
        forward[chunk] = copies.start(other_quarter, other_quarter, near)

    def finish(chunk):
        around[chunk][1].wait_recv()
        forward[chunk].wait_recv()

    def pieces(act):
        def both(chunk):
            act(2 * chunk)
            act(2 * chunk + 1)

        return both

    stages = [pieces(first)]
    stages += [pieces(lambda piece, level=level: later(piece, level)) for level in range(lower)]
    stages += [pieces(send_near), send_far, sum_far, pass_on, finish]
    extra = {1: [vec_begin], len(stages) - 3: [slots.begin]}
    for level in range(bits):
        tick = min(3 + 2 * level, CHUNKS + len(stages) - 2)
        extra.setdefault(tick, []).append(functools.partial(vecs.advance, level))
        tick = min(len(stages) - 1 + level, CHUNKS + len(stages) - 2)
        extra.setdefault(tick, []).append(functools.partial(slots.advance, level))
    for tick in range(CHUNKS + len(stages) - 1):
        for stage in reversed(range(len(stages))):
            place = tick - stage
            if 0 <= place < CHUNKS:
                stages[stage](ORDER[place])
        for act in extra.get(tick, ()):
            act()
    for copy in field_copies:
        copy.wait_recv()
    copies.finish()


def reduce_all(count, groups, grads, slots, vec, field):
    bits = count.bit_length() - 1
    lower = bits - 1
    rows = grads.shape[3]
    half = CHUNK // 2
    pieces = 2 * CHUNKS
    share = CHUNK // groups
    copies = 2 * (groups - 1) + pieces * (bits + 1) + 4 * CHUNKS + 2 + 2 * (count - 1)
    bfloat = jnp.bfloat16
    vmem = pl.BlockSpec(memory_space=pltpu.VMEM)
    return pl.pallas_call(
        functools.partial(reduce_kernel, count, groups),
        out_shape=(
            jax.ShapeDtypeStruct((CHUNKS, groups, share, rows, WIDTH), bfloat),
            jax.ShapeDtypeStruct((count, rows, WIDTH), jnp.float32),
            jax.ShapeDtypeStruct((count, groups) + vec.shape, jnp.float32),
            jax.ShapeDtypeStruct(field.shape, field.dtype),
        ),
        in_specs=[vmem] * 4,
        out_specs=(vmem,) * 4,
        scratch_shapes=[
            pltpu.VMEM((pieces, half, count // 2, rows, WIDTH), bfloat),
            pltpu.VMEM((pieces, count // 4, half, rows, WIDTH), jnp.float32),
            pltpu.VMEM((pieces, count // 2 - 1, half, rows, WIDTH), bfloat),
            pltpu.VMEM((pieces, count // 2 - 1, half, rows, WIDTH), bfloat),
            pltpu.VMEM((pieces, share, rows, WIDTH), bfloat),
            pltpu.VMEM((pieces, share, rows, WIDTH), bfloat),
            pltpu.VMEM((pieces, share, rows, WIDTH), jnp.float32),
            pltpu.VMEM((CHUNKS, share, rows, WIDTH), bfloat),
            pltpu.VMEM((CHUNKS, share, rows, WIDTH), bfloat),
            pltpu.SemaphoreType.DMA((copies,)),
            pltpu.SemaphoreType.DMA((copies,)),
        ],
        compiler_params=pltpu.CompilerParams(
            collective_id=0, has_side_effects=True, vmem_limit_bytes=60 << 20
        ),
    )(grads, slots, vec, field)


def pack_rows(blocks, count, rows):
    own = blocks.shape[1] // count
    blocks = blocks.reshape(blocks.shape[0], count // 2, 2, own, WIDTH)
    return jnp.pad(blocks, ((0, 0), (0, 0), (0, 0), (0, rows - own), (0, 0)))


def renew_into(outs, refs, at, gradient, step_rate):
    new = renew(*(ref[at] for ref in refs), gradient, step_rate)
    for out, value in zip(outs, new):
        out[at] = value


def update_kernel(groups, sum_ref, slot_ref, vec_ref, *refs):
    flt = jnp.float32
    slot_in, square_in, wide_in, mlp_in, vector_in = (refs[3 * i : 3 * i + 3] for i in range(5))
    refs = refs[15:]
    slot_out, square_out, wide_out, mlp_out, vector_out = (
        refs[4 * i : 4 * i + 4] for i in range(5)
    )
    own = wide_in[0].shape[0]
    bfloat = jnp.bfloat16
    last = CHUNKS - 1

    def block(place):
        if place < last * CHUNK:
            chunk, rest = divmod(place, CHUNK)
            share = CHUNK // groups
        else:
            chunk, rest, share = last, place - last * CHUNK, CHUNK // groups - 1
        return sum_ref[chunk, rest // share, rest % share, :own]

    for place in range(12):
        part = (slice(None), slice(place * WIDTH, (place + 1) * WIDTH))
        for half in range(2):
            grads = block(12 * half + place).astype(flt)
            renew_into(mlp_out, mlp_in, (half,) + part, grads, RATE)
    for place in range(9):
        part = (slice(None), slice(place * WIDTH, (place + 1) * WIDTH))
        renew_into(wide_out, wide_in, part, block(24 + place).astype(flt), RATE)
    for which, base in ((3, 33), (2, 36), (1, 39)):
        for place in range(3):
            part = (which, slice(None), slice(place * WIDTH, (place + 1) * WIDTH))
            renew_into(square_out, square_in, part, block(base + place).astype(flt), RATE)
    asked = vector_in[0][0:1]
    lane = lax.broadcasted_iota(jnp.int32, (WIDTH, D), 1) // HDIM
    head = lax.broadcasted_iota(jnp.int32, (WIDTH, D), 0)
    asked_high, asked_low = halves(jnp.where(lane == head, asked, 0.0))
    keys = block(42)
    renew_into(
        square_out, square_in, (0,), matmul(keys, asked_high) + matmul(keys, asked_low), RATE
    )
    devices = vec_ref.shape[0]
    pick = lax.broadcasted_iota(jnp.int32, (D, own), 0) == lax.axis_index(
        "dp"
    ) * own + lax.broadcasted_iota(jnp.int32, (D, own), 1)
    conditions = matmul(vec_ref[:, 11, :].astype(bfloat), jnp.where(pick, 1.0, 0.0).astype(bfloat))
    conditions = conditions.T.astype(bfloat)
    for row in range(6):
        high, low = halves(vec_ref[:, 5 + row, :])
        part = (slice(None), slice((3 + row) * D, (4 + row) * D))
        grads = matmul(conditions, high) + matmul(conditions, low)
        renew_into(wide_out, wide_in, part, grads, RATE)
    total = vec_ref[0]
    for device in range(1, devices):
        total = total + vec_ref[device]
    renew_into(vector_out, vector_in, (slice(None),), total[:11], RATE)
    each = slot_in[0].shape[1]
    blocks = slot_ref.shape[0]
    size = slot_share((PATCH + 1) * each, blocks)
    flat = jnp.concatenate([slot_ref[b, :size] for b in range(blocks)], axis=0)
    for p in range(PATCH + 1):
        pieces = [
            flat[(piece * (PATCH + 1) + p) * each : (piece * (PATCH + 1) + p + 1) * each]
            for piece in range(3)
        ]
        renew_into(slot_out, slot_in, (p,), jnp.concatenate(pieces, axis=1), EMBED_RATE)


def update_all(groups, sums, slot_blocks, vec_all, parameters):
    vmem = pl.BlockSpec(memory_space=pltpu.VMEM)
    shapes = [jax.ShapeDtypeStruct(a.shape, a.dtype) for a in parameters[::3] for _ in range(4)]
    return pl.pallas_call(
        functools.partial(update_kernel, groups),
        out_shape=tuple(shapes),
        in_specs=[vmem] * (3 + len(parameters)),
        out_specs=(vmem,) * len(shapes),
        compiler_params=pltpu.CompilerParams(vmem_limit_bytes=60 << 20),
    )(sums, slot_blocks, vec_all, *parameters)


def gather_kernel(
    count,
    groups,
    field_ref,
    slot_ref,
    ident_ref,
    cond_ref,
    square_ref,
    wide_ref,
    mlp_ref,
    vec_ref,
    patch_out,
    slots_out,
    mask_out,
    cols_out,
    square_out,
    qkv_out,
    mlp_out,
    field_all,
    slot_all,
    ident_all,
    cond_all,
    part,
    part_in,
    send_sem,
    recv_sem,
):
    bfloat, flt = jnp.bfloat16, jnp.float32
    bits = count.bit_length() - 1
    dp, here = lax.axis_index("dp"), lax.axis_index("vars")
    own, rows = square_ref.shape[1], square_out.shape[2]
    if own < rows:
        square_out[:, dp] = jnp.zeros_like(square_out[:, dp])
        qkv_out[dp] = jnp.zeros_like(qkv_out[dp])
        mlp_out[:, dp] = jnp.zeros_like(mlp_out[:, dp])
    square_out[:, dp, :own] = square_ref[...].astype(bfloat)
    qkv_out[dp, :own] = wide_ref[:, : 3 * D].astype(bfloat)
    mlp_out[:, dp, :own] = mlp_ref[...].astype(bfloat)
    cond_all[dp] = cond_ref[...]
    greet(dp, here, range(1, count), bits, groups)
    copies = Copies(send_sem, recv_sem)
    most = PATCH // 2 + 1
    forth = list(range(1, bits)) + [0]
    back = list(range(1, bits))[::-1] + [0]
    ones = Spread(
        copies,
        [lambda block: square_out.at[:, block], lambda block: qkv_out.at[block]],
        dp,
        bits,
        forth,
    )
    twos = Spread(copies, [lambda block: mlp_out.at[:, block]], dp, bits, back)
    conds = [
        copies.start(cond_ref, cond_all.at[dp], {"dp": (dp + step) % count})
        for step in range(1, count)
    ]
    core = dp % 2
    arrivals, slot_copies = [], []
    sent = pl.ds(core * (PATCH + 1 - most), most)
    for step in range(1, groups):
        to = {"vars": (here + step) % groups}
        arrivals.append(copies.start(ident_ref, ident_all.at[here], to))
        slot_copies.append(copies.start(slot_ref.at[sent], slot_all.at[here, sent], to))
    ones.begin()
    twos.begin()
    for step in range(1, groups):
        to = (here + step) % groups
        arrivals.append(copies.start(field_ref.at[to], field_all.at[here], {"vars": to}))
    field_all[here] = field_ref[here]
    slot_all[here] = slot_ref[...]
    ident_all[here] = ident_ref[...]
    for copy in conds:
        copy.wait_recv()
    cond = cond_all[:, 0, :].astype(bfloat)
    pick = lax.broadcasted_iota(jnp.int32, (D, own), 0) == dp * own + lax.broadcasted_iota(
        jnp.int32, (D, own), 1
    )
    cond_rows = matmul(cond, jnp.where(pick, 1.0, 0.0).astype(bfloat)).astype(bfloat)
    shares = matmul(cond_rows, wide_ref[:, 3 * D :].astype(bfloat))
    strips = shares.shape[1] // WIDTH
    for block in range(count):
        for strip in range(strips):
            part[block, strip : strip + 1] = shares[
                block : block + 1, strip * WIDTH : (strip + 1) * WIDTH
            ]
    part_copies = [
        copies.start(part.at[(dp + step) % count], part_in.at[step - 1], {"dp": (dp + step) % count})
        for step in range(1, count)
    ]
    ones.advance(0)
    twos.advance(0)
    fewer = PATCH + 1 - most
    given = pl.ds(core * most, fewer)
    for step, copy in enumerate(slot_copies, 1):
        copy.wait_recv()
        block = slot_all.at[(here - step + groups) % groups, given]
        arrivals.append(copies.start(block, block, {"dp": dp + 1 - 2 * core}))
    for level in range(1, bits):
        ones.advance(level)
        twos.advance(level)
    for copy in part_copies:
        copy.wait_recv()
    mine = part[dp]
    for step in range(1, count):
        mine = mine + part_in[step - 1]
    wide_parts = [
        jnp.concatenate([mine[3 * row + strip : 3 * row + strip + 1] for strip in range(3)], axis=1)
        for row in range(6)
    ]
    modulation = jnp.concatenate(wide_parts, axis=0) + vec_ref[5:11]
    columns = jnp.concatenate(
        [
            vec_ref[1:5],
            modulation,
            vec_ref[0:1],
            cond_ref[0:1],
            jnp.zeros((WIDTH - 12, D), flt),
        ],
        axis=0,
    )
    cols_out[...] = columns.T
    for copy in arrivals:
        copy.wait_recv()
    each = slot_ref.shape[1]
    spare = SLOT_ROWS - groups * each
    for p in range(PATCH):
        pieces = [
            field_all[source, p * each : (p + 1) * each].astype(flt) for source in range(groups)
        ]
        pieces.append(jnp.zeros((spare, field_ref.shape[2]), flt))
        patch_out[p] = jnp.concatenate(pieces, axis=0).astype(bfloat)
    for p in range(PATCH + 1):
        pieces = [slot_all[source, p] for source in range(groups)]
        pieces.append(jnp.zeros((spare, D), flt))
        slots_out[p * SLOT_ROWS : (p + 1) * SLOT_ROWS] = jnp.concatenate(pieces, axis=0)
    pieces = [ident_all[source, :each] for source in range(groups)]
    pieces.append(jnp.full((spare, WIDTH), float(NVARS), flt))
    mask_out[...] = jnp.where(jnp.concatenate(pieces, axis=0) < NVARS, 0.0, FAR)
    copies.finish()


def gather_all(count, groups, field, slots, ident, cond, square, wide, mlp, vectors):
    bits = count.bit_length() - 1
    own = square.shape[1]
    rows = -(-own // 16) * 16
    bfloat, flt = jnp.bfloat16, jnp.float32
    copies = 4 * (groups - 1) + 5 * (count - 1)
    length = field.shape[2]
    strips = (wide.shape[1] - 3 * D) // WIDTH
    vmem = pl.BlockSpec(memory_space=pltpu.VMEM)
    outs = [
        ((PATCH, SLOT_ROWS, length), bfloat),
        (((PATCH + 1) * SLOT_ROWS, D), flt),
        ((SLOT_ROWS, WIDTH), flt),
        ((D, WIDTH), flt),
        ((4, count, rows, D), bfloat),
        ((count, rows, 3 * D), bfloat),
        ((2, count, rows, 4 * D), bfloat),
    ]
    return pl.pallas_call(
        functools.partial(gather_kernel, count, groups),
        out_shape=tuple(jax.ShapeDtypeStruct(shape, dtype) for shape, dtype in outs),
        in_specs=[vmem] * 8,
        out_specs=(vmem,) * len(outs),
        scratch_shapes=[
            pltpu.VMEM((groups,) + field.shape[1:], bfloat),
            pltpu.VMEM((groups,) + slots.shape, flt),
            pltpu.VMEM((groups,) + ident.shape, flt),
            pltpu.VMEM((count, 8, D), flt),
            pltpu.VMEM((count, strips, WIDTH), flt),
            pltpu.VMEM((count - 1, strips, WIDTH), flt),
            pltpu.SemaphoreType.DMA((copies,)),
            pltpu.SemaphoreType.DMA((copies,)),
        ],
        compiler_params=pltpu.CompilerParams(
            collective_id=1, has_side_effects=True, vmem_limit_bytes=60 << 20
        ),
    )(field, slots, ident, cond, square, wide, mlp, vectors)


def on_device(
    fields,
    var_ids,
    segments,
    condition,
    cotangent,
    slot_weights,
    slot_momentum,
    slot_average,
    square,
    square_momentum,
    square_average,
    wide,
    wide_momentum,
    wide_average,
    mlp,
    mlp_momentum,
    mlp_average,
    vectors,
    vectors_momentum,
    vectors_average,
):
    bfloat = jnp.bfloat16
    length = fields.shape[4]
    count, groups = lax.axis_size("dp"), lax.axis_size("vars")
    own = square.shape[1]
    rows = -(-own // 16) * 16
    cond_low = jax.nn.silu(condition[0].astype(jnp.float32)).astype(bfloat).astype(jnp.float32)
    field = jnp.transpose(fields[:, 0], (1, 2, 0, 3)).reshape(groups, -1, length)
    field = jnp.pad(field, ((0, 0), (0, -field.shape[1] % 16), (0, 0)))
    ident = jnp.broadcast_to(var_ids.astype(jnp.float32)[:, None], (slot_weights.shape[0], WIDTH))
    gathered = gather_all(
        count,
        groups,
        field,
        jnp.transpose(slot_weights, (1, 0, 2)),
        ident,
        jnp.broadcast_to(cond_low, (8, D)),
        square,
        wide,
        mlp,
        vectors,
    )
    patches, slot_rows, mask, columns = gathered[:4]
    square_full, qkv_full, mlp_full = (a[..., :own, :] for a in gathered[4:])
    block_out, grads, slots_packed, vec, field = block_step(
        count,
        groups,
        own,
        slot_weights.shape[0],
        segments[0],
        patches,
        slot_rows,
        mask,
        square_full.reshape(4, D, D),
        qkv_full.reshape(D, 3 * D),
        mlp_full.reshape(2, D, 4 * D),
        columns,
        cotangent[0, 0],
    )
    sums, slot_blocks, vec_all, field_back = reduce_all(
        count, groups, pack_rows(grads, count, rows), slots_packed, vec, field
    )
    updated = update_all(
        groups,
        sums,
        slot_blocks,
        vec_all.reshape(-1, VEC_ROWS, D),
        (
            *(jnp.transpose(a, (1, 0, 2)) for a in (slot_weights, slot_momentum, slot_average)),
            square,
            square_momentum,
            square_average,
            wide,
            wide_momentum,
            wide_average,
            mlp,
            mlp_momentum,
            mlp_average,
            vectors,
            vectors_momentum,
            vectors_average,
        ),
    )
    each = slot_weights.shape[0]
    field_back = field_back[:, : PATCH * each].reshape(groups, PATCH, each, length)
    field_grad = jnp.transpose(field_back, (2, 0, 1, 3)).astype(jnp.float32)[:, None]
    slot_new = tuple(jnp.transpose(a, (1, 0, 2)) for a in updated[:4])
    return (block_out[None, None], field_grad) + slot_new + tuple(updated[4:])


def solution(mesh):
    placed = (
        P("vars", "dp", None, None, None),
        P("vars"),
        P("dp", "vars", None),
        P("dp", "vars", None),
        P("dp", "vars", None, None),
        P("vars", None, None),
        P("vars", None, None),
        P("vars", None, None),
        P(None, "dp", None),
        P(None, "dp", None),
        P(None, "dp", None),
        P("dp", None),
        P("dp", None),
        P("dp", None),
        P(None, "dp", None),
        P(None, "dp", None),
        P(None, "dp", None),
        P(),
        P(),
        P(),
    )
    return jax.shard_map(
        on_device,
        mesh=mesh,
        in_specs=placed,
        out_specs=(
            P("dp", "vars", None, None),
            P("vars", "dp", None, None, None),
            P("vars", None, None),
            P("vars", None, None),
            P("vars", None, None),
            P("vars", None, None),
            P(None, "dp", None),
            P(None, "dp", None),
            P(None, "dp", None),
            P(None, "dp", None),
            P("dp", None),
            P("dp", None),
            P("dp", None),
            P("dp", None),
            P(None, "dp", None),
            P(None, "dp", None),
            P(None, "dp", None),
            P(None, "dp", None),
            P(),
            P(),
            P(),
            P(),
        ),
        check_vma=False,
    )
```

profile of v0, /device:TPU:0, one launch (start us, length us, event | category | flops | bytes accessed | tf_op | source)
XLA Modules:
  0.0 187.2 jit_solution(11970695815623002826)
XLA Ops:
  0.7 0.7 convert_element_type.39
  1.3 0.7 convert_reduce_fusion
  2.0 0.6 broadcast_in_dim.21.cond_ref
  2.6 0.7 broadcast_in_dim.20.ident_ref
  3.3 1.4 copy.44
  4.7 0.2 copy.45
  4.9 0.9 pad.4.field_ref
  5.8 34.2 %shard_map.363 = (bf16[4,80,1024]{2,1,0:T(8,128)(2,1)}, f32[400,384]{1,0:T(8,128)}, f32[80,128]{1,0:T(8,128)}, f32[384,128]{1,0:T(8,128)}, bf16[4,8,48,384]{3,2,...) custom-call(bf16[4,80,1024]{2,1,0:T(8,128)(2,1)} %pad.4.field_ref, ...), custom_call_target="tpu_custom_call" | custom-call | tf_op jit(solution)/shard_map/pallas_call | solution.py:1134
  40.0 78.8 %shard_map.364 = (bf16[1024,384]{1,0:T(8,128)(2,1)}, bf16[44,384,128]{2,1,0:T(8,128)(2,1)}, bf16[4,4,2,48,128]{4,3,2,1,0:T(8,128)(2,1)}, f32[16,384]{1,0:T(8,128)}, bf16[4,80,1024]{2,1,0:T(8,128)(2,1)}) custom-call(s32[1,1024]{1,0:T(1,128)} %bitcast.37, bf16[4,80,1024]{2,1,0:T(8,128)(2,1)} %get-tuple-element.58.fields_ref, ...), custom_call_target="tpu_custom_call" | custom-call | tf_op jit(solution)/shard_map/pallas_call | solution.py:537
  118.7 57.1 %shard_map.365 = (bf16[4,4,3,48,128]{4,3,2,1,0:T(8,128)(2,1)}, f32[8,48,128]{2,1,0:T(8,128)}, f32[8,4,16,384]{3,2,1,0:T(8,128)}, bf16[4,80,1024]{2,1,0:T(8,128)(2,1)}) custom-call(bf16[44,4,2,48,128]{4,3,2,1,0:T(8,128)(2,1)} %bitcast.25, bf16[4,4,2,48,128]{4,3,2,1,0:T(8,128)(2,1)} %get-tuple-element.67.s_ref, f32[16,384]{1,0:T(8,128)} %get-tuple-element.68.vec_ref, ...), custom_call_target="tpu_custom_call" | custom-call | tf_op jit(solution)/shard_map/pallas_call | solution.py:856
  175.8 1.2 slice_convert_fusion
  177.0 0.8 copy.46
  177.8 1.9 copy.47
  179.6 7.4 %shard_map.366 = (f32[5,18,384]{2,1,0:T(8,128)}, f32[5,18,384]{2,1,0:T(8,128)}, f32[5,18,384]{2,1,0:T(8,128)}, f32[5,18,384]{2,1,0:T(8,128)}, f32[4,48,384]{2,1,...) custom-call(bf16[4,4,3,48,128]{4,3,2,1,0:T(8,128)(2,1)} %get-tuple-e, ...), custom_call_target="tpu_custom_call" | custom-call | tf_op jit(solution)/shard_map/pallas_call | solution.py:966
  (1 shorter events, 0.0 us)
where the time goes:
time: 188 us; the launch traced here: 187 us
  Pallas kernels  177 us (94%)
  local copies, waits for them, and re-layouts  6.35 us (3%)
  other arithmetic  2.56 us (1%)
    pallas_call x1, Pallas kernels, block_step(): pl.pallas_call(functools.partial(block_kernel, groups * count * length, g...  78.8 us
    pallas_call x1, Pallas kernels, reduce_all(): pl.pallas_call(functools.partial(reduce_kernel, count, groups), out_shape...  57.1 us
    pallas_call x1, Pallas kernels, gather_all(): pl.pallas_call(functools.partial(gather_kernel, count, groups), out_shape...  34.2 us
    pallas_call x1, Pallas kernels, update_all(): pl.pallas_call(functools.partial(update_kernel, groups), out_shape=tuple(...  7.36 us

commit v1 on v0

--- a/solution.py
+++ b/solution.py
@@ -75,12 +75,12 @@
     mask_ref,
     square_ref,
     qkv_ref,
-    mlp_ref,
+    mlp_hbm,
     cols_ref,
     segment_ref,
-    cot_ref,
-    out_ref,
-    grad_ref,
+    cot_hbm,
+    out_hbm,
+    grad_hbm,
     slot_ref,
     vec_ref,
     field_ref,
@@ -120,14 +120,27 @@
     key_acc,
     column_acc,
     keyvec_ref,
+    mlp_ref,
+    cot_ref,
+    out_rows,
+    grad_rows,
     spans_ref,
+    in_sem,
+    out_sem,
 ):
     bfloat, flt = jnp.bfloat16, jnp.float32
+    loads = [
+        pltpu.make_async_copy(mlp_hbm, mlp_ref, in_sem.at[0]),
+        pltpu.make_async_copy(cot_hbm, cot_ref, in_sem.at[1]),
+    ]
+    for load in loads:
+        load.start()
     length = cot_ref.shape[0]
     tiles = length // TILE
     depth = D
     each = slots_each
     team_size = raw.shape[1]
+    spread = 2 if team_size == HEADS else 1
     scale = HDIM ** (-0.5)
 
     def lanes(i):
@@ -141,10 +154,6 @@
     for block in range(3):
         part = slice(block * depth, (block + 1) * depth)
         qkv_t[part] = qkv_ref[:, part].astype(flt).T.astype(bfloat)
-    for block in range(4):
-        part = slice(block * depth, (block + 1) * depth)
-        up_t[part] = mlp_ref[0, :, part].astype(flt).T.astype(bfloat)
-        down_t[part] = mlp_ref[1, :, part].astype(flt).T.astype(bfloat)
     asked = cols_ref[:, 10:11]
     lane = lax.broadcasted_iota(jnp.int32, (depth, WIDTH), 1)
     head_of = lax.broadcasted_iota(jnp.int32, (depth, WIDTH), 0) // HDIM
@@ -181,6 +190,12 @@
     key_acc[...] = jnp.zeros_like(key_acc)
     grad_triple[...] = jnp.zeros_like(grad_triple)
 
+    packed = field_ref.shape[1]
+    target = lax.broadcasted_iota(jnp.int32, (packed, packed), 0)
+    origin = lax.broadcasted_iota(jnp.int32, (packed, packed), 1)
+    place = (target % PATCH) * each + target // PATCH
+    arrange = jnp.where((origin == place) & (target < PATCH * each), 1.0, 0.0).astype(bfloat)
+
     def fields_at(i):
         return [fields_ref[p, :, lanes(i)].astype(flt) for p in range(PATCH)]
 
@@ -200,7 +215,7 @@
         second = jnp.mean(grad * normed, axis=0, keepdims=True)
         return inv * (grad - first - normed * second)
 
-    @pl.loop(0, tiles)
+    @pl.loop(0, tiles, unroll=spread)
     def _(i):
         at = lanes(i)
         fields = fields_at(i)
@@ -226,17 +241,18 @@
         ident = lax.broadcasted_iota(jnp.int32, (AUGMENT - HDIM, TILE), 0)
         hot = jnp.where(ident == segment, 1.0, 0.0)
         cold = jnp.where((ident != segment) & (ident < 4), FAR, 0.0)
+        triples = [
+            matmul(qkv_t[block * depth : (block + 1) * depth], low).astype(bfloat)
+            for block in range(3)
+        ]
+        key_t[:, at] = triples[1]
         for head in range(HEADS):
             part = slice(head * HDIM, (head + 1) * HDIM)
-            queries = matmul(qkv_t[part], low).astype(bfloat).astype(flt) * scale
+            queries = triples[0][part].astype(flt) * scale
             query[head, :, at] = jnp.concatenate([queries, hot], axis=0).astype(bfloat)
-            part = slice(depth + head * HDIM, depth + (head + 1) * HDIM)
-            keys = matmul(qkv_t[part], low).astype(bfloat)
-            key_t[head * HDIM : (head + 1) * HDIM, at] = keys
-            long = jnp.concatenate([keys.astype(flt), cold], axis=0)
+            long = jnp.concatenate([triples[1][part].astype(flt), cold], axis=0)
             key[head, at] = long.T.astype(bfloat)
-            part = slice(2 * depth + head * HDIM, 2 * depth + (head + 1) * HDIM)
-            values = matmul(qkv_t[part], low).astype(bfloat)
+            values = triples[2][part]
             value[head, at] = values.astype(flt).T.astype(bfloat)
             value_t[head, :HDIM, at] = values
             value_t[head, HDIM:, at] = jnp.ones((AUGMENT - HDIM, TILE), bfloat)
@@ -281,6 +297,12 @@
                 log_sum[head : head + 1, at] = tops[head - base] + jnp.log(totals[head - base])
 
     rate = 1.0 / math.sqrt(tokens_all)
+    for load in loads:
+        load.wait()
+    for block in range(4):
+        part = slice(block * depth, (block + 1) * depth)
+        up_t[part] = mlp_ref[0, :, part].astype(flt).T.astype(bfloat)
+        down_t[part] = mlp_ref[1, :, part].astype(flt).T.astype(bfloat)
 
     @pl.loop(0, tiles)
     def _(i):
@@ -304,10 +326,10 @@
                 GELU_ROOT + (3.0 * GELU_ROOT * GELU_CUBE) * square
             )
             raw[block // team_size, block % team_size] = slope
-            out = out + matmul(mlp_ref[1, :, part], act)
+        out = out + matmul(mlp_ref[1], active[:, at])
         result = mid + column(9) * out
         rows = pl.ds(pl.multiple_of(i * TILE, TILE), TILE)
-        out_ref[rows] = result.T.astype(bfloat)
+        out_rows[rows] = result.T.astype(bfloat)
         grad = cot_ref[rows].astype(flt).T * rate
         column_acc[9] += fold(grad * out)
         low_grad = (grad * column(9)).astype(bfloat)
@@ -342,11 +364,23 @@
             grads = contract_cols(left[...], right[block : block + size])
             for piece in range(size // WIDTH):
                 place = base + block // WIDTH + piece
-                grad_ref[place] = grads[:, piece * WIDTH : (piece + 1) * WIDTH].astype(bfloat)
+                grad_rows[place] = grads[:, piece * WIDTH : (piece + 1) * WIDTH].astype(bfloat)
 
     weight_grad(input_two, grad_up, 4 * depth, 0)
     weight_grad(grad_branch, active, 4 * depth, 12)
     weight_grad(attended, grad_att, depth, 33)
+    stores = [pltpu.make_async_copy(out_rows, out_hbm, out_sem.at[0])]
+
+    def store_grads(first, past):
+        part = pl.ds(first, past - first)
+        stores.append(
+            pltpu.make_async_copy(grad_rows.at[part], grad_hbm.at[part], out_sem.at[len(stores)])
+        )
+        stores[-1].start()
+
+    stores[0].start()
+    store_grads(0, 24)
+    store_grads(33, 36)
 
     @pl.loop(0, tiles)
     def _(i):
@@ -355,21 +389,25 @@
         @pl.loop(spans_ref[i, 0], spans_ref[i, 1])
         def _(j):
             to = lanes(j)
+            parts = [slice(head * HDIM, (head + 1) * HDIM) for head in range(HEADS)]
+            logits = [matmul(key[head, to], query[head, :, at]) for head in range(HEADS)]
+            backs = [matmul(value[head, to], grad_out[parts[head], at]) for head in range(HEADS)]
+            weights = [jnp.exp(logits[h] - log_sum[h : h + 1, at]) for h in range(HEADS)]
+            grad_raw = [
+                (weights[h] * (backs[h] - inner[h : h + 1, at])).astype(bfloat)
+                for h in range(HEADS)
+            ]
+            weights = [weight.astype(bfloat) for weight in weights]
+            for head, part in enumerate(parts):
+                grad_triple[part, at] += matmul(key_t[part, to], grad_raw[head])
             for head in range(HEADS):
-                part = slice(head * HDIM, (head + 1) * HDIM)
-                queries = query[head, :, at]
-                logits = matmul(key[head, to], queries)
-                prob = jnp.exp(logits - log_sum[head : head + 1, at])
-                grads = grad_out[part, at]
-                back = matmul(value[head, to], grads)
-                grad_raw = (prob * (back - inner[head : head + 1, at])).astype(bfloat)
-                grad_triple[part, at] += matmul(key_t[part, to], grad_raw)
                 part = slice(depth + head * HDIM, depth + (head + 1) * HDIM)
-                grad_triple[part, to] += contract_cols(queries[:HDIM], grad_raw)
+                grad_triple[part, to] += contract_cols(query[head, :HDIM, at], grad_raw[head])
+            for head in range(HEADS):
                 part = slice(2 * depth + head * HDIM, 2 * depth + (head + 1) * HDIM)
-                grad_triple[part, to] += contract_cols(grads, prob.astype(bfloat))
-
-    @pl.loop(0, tiles)
+                grad_triple[part, to] += contract_cols(grad_out[parts[head], at], weights[head])
+
+    @pl.loop(0, tiles, unroll=spread)
     def _(i):
         at = lanes(i)
         grad_in = jnp.zeros((depth, TILE), flt)
@@ -380,7 +418,7 @@
                 grads = grads * scale
             grads = grads.astype(bfloat)
             active[part, at] = grads
-            grad_in = grad_in + matmul(qkv_ref[:, part], grads)
+        grad_in = matmul(qkv_ref[...], active[: 3 * depth, at])
         inv = inverse[0:1, at]
         begin = start[:, at]
         normed = (begin - jnp.mean(begin, axis=0, keepdims=True)) * inv
@@ -415,9 +453,12 @@
         for group in range(groups):
             pieces = [grad[group * each : (group + 1) * each] for grad in field_grads]
             pieces.append(jnp.zeros((field_ref.shape[1] - PATCH * each, TILE), flt))
-            field_ref[group, :, at] = jnp.concatenate(pieces, axis=0).astype(bfloat)
+            field_ref[group, :, at] = matmul(
+                arrange, jnp.concatenate(pieces, axis=0).astype(bfloat)
+            ).astype(bfloat)
 
     weight_grad(input_one, active, 3 * depth, 24)
+    store_grads(24, 33)
     weight_grad(pooled, attended, depth, 36)
     maps_high, maps_low = halves(map_acc[...])
     value_grad = (
@@ -427,7 +468,7 @@
     )
     for piece in range(3):
         part = slice(piece * WIDTH, (piece + 1) * WIDTH)
-        grad_ref[39 + piece] = value_grad[:, part].astype(bfloat)
+        grad_rows[39 + piece] = value_grad[:, part].astype(bfloat)
     lane = lax.broadcasted_iota(jnp.int32, (SLOT_ROWS, WIDTH), 1)
     keys = []
     for p in range(PATCH + 1):
@@ -442,8 +483,9 @@
     key_grad = (
         matmul(slots_t[0], keys_high) + matmul(slots_t[0], keys_low) + matmul(slots_t[1], keys_high)
     )
-    grad_ref[42] = key_grad.astype(bfloat)
-    grad_ref[43] = jnp.zeros_like(grad_ref[43])
+    grad_rows[42] = key_grad.astype(bfloat)
+    grad_rows[43] = jnp.zeros_like(grad_rows[43])
+    store_grads(36, 44)
     slot_grad = (
         matmul(value_weight, maps_high)
         + matmul(value_weight, maps_low)
@@ -481,6 +523,8 @@
             lane == which + 1, jnp.sum(column_acc[which], axis=1, keepdims=True), 0.0
         )
     vec_ref[...] = columns.T[:VEC_ROWS]
+    for store in stores:
+        store.wait()
 
 
 def slot_share(rows, count):
@@ -496,6 +540,7 @@
     field_rows = -(-PATCH * each // 16) * 16
     team_size = HEADS if count * block_rows <= D else HEADS // 2
     vmem = pl.BlockSpec(memory_space=pltpu.VMEM)
+    hbm = pl.BlockSpec(memory_space=pl.ANY)
     shapes = [
         ((D, D), bfloat),
         ((3 * D, D), bfloat),
@@ -533,6 +578,10 @@
         ((HEADS, PATCH + 1, SLOT_ROWS, WIDTH), flt),
         ((10, D, WIDTH), flt),
         ((D, WIDTH), bfloat),
+        ((2, D, 4 * D), bfloat),
+        ((length, D), bfloat),
+        ((length, D), bfloat),
+        ((44, D, WIDTH), bfloat),
     ]
     return pl.pallas_call(
         functools.partial(block_kernel, groups * count * length, groups, each),
@@ -543,10 +592,16 @@
             jax.ShapeDtypeStruct((VEC_ROWS, D), flt),
             jax.ShapeDtypeStruct((groups, field_rows, length), bfloat),
         ),
-        in_specs=[pl.BlockSpec(memory_space=pltpu.SMEM)] + [vmem] * 9,
-        out_specs=(vmem,) * 5,
+        in_specs=[pl.BlockSpec(memory_space=pltpu.SMEM)]
+        + [vmem] * 5
+        + [hbm, vmem, vmem, hbm],
+        out_specs=(hbm, hbm, vmem, vmem, vmem),
         scratch_shapes=[pltpu.VMEM(shape, dtype) for shape, dtype in shapes]
-        + [pltpu.SMEM((tiles, 2), jnp.int32)],
+        + [
+            pltpu.SMEM((tiles, 2), jnp.int32),
+            pltpu.SemaphoreType.DMA((2,)),
+            pltpu.SemaphoreType.DMA((5,)),
+        ],
         compiler_params=pltpu.CompilerParams(vmem_limit_bytes=62 << 20),
     )(segment, fields, slots, mask, square, qkv, mlp, cols, segment, cot)
 
@@ -618,8 +673,9 @@
 
 
 class Spread:
-    def __init__(self, copies, refs, dp, bits, order):
+    def __init__(self, copies, refs, dp, bits, order, own=None):
         self.copies, self.refs, self.dp, self.bits = copies, refs, dp, bits
+        self.own = own
         self.order = order
         self.arriving = {}
 
@@ -628,8 +684,9 @@
         for level in range(first, len(self.order)):
             bit = self.order[level]
             partner = {"dp": flip(self.dp, 1 << bit, self.bits)}
-            for ref in self.refs:
-                copy = self.copies.start(ref(block), ref(block), partner)
+            for which, ref in enumerate(self.refs):
+                source = self.own[which] if self.own and not mask else ref(block)
+                copy = self.copies.start(source, ref(block), partner)
                 self.arriving.setdefault(level, []).append((mask | (1 << bit), copy))
 
     def begin(self):
@@ -662,6 +719,10 @@
     zkeep,
     ysend,
     yrecv,
+    lsend,
+    lrecv,
+    g_own,
+    own_sem,
     send_sem,
     recv_sem,
 ):
@@ -669,6 +730,8 @@
     lower = bits - 1
     dp, here = lax.axis_index("dp"), lax.axis_index("vars")
     core, pair = dp % 2, dp // 2
+    own_copy = pltpu.make_async_copy(g_ref.at[:, :, core], g_own, own_sem.at[0])
+    own_copy.start()
     greet(dp, here, [1 << bit for bit in range(bits)], bits, groups)
     copies = Copies(send_sem, recv_sem)
     half = CHUNK // 2
@@ -725,6 +788,7 @@
         vecs.begin()
 
     crossing = {}
+    own_copy.wait()
 
     def send_level(piece, level):
         order = rounds_of(lower, piece % 2)
@@ -745,7 +809,7 @@
         kept = 2 ** (lower - 1)
         for entry in range(2**lower):
             block = flip(pair, mask_of(order, 0, entry), lower)
-            value = g_ref[pl.ds(base, size), block, core].astype(jnp.float32)
+            value = g_own[pl.ds(base, size), block].astype(jnp.float32)
             value = value + recv0[piece, pl.ds(0, size), block].astype(jnp.float32)
             if size < half:
                 rest = half - size
@@ -777,7 +841,11 @@
     low, top = here % 2, here // 2
     across, over, around, forward = {}, {}, {}, {}
 
+    final = ORDER[-1]
+
     def send_near(piece):
+        if piece // 2 == final:
+            return
         zsend[piece] = acc[piece, 0, pl.ds(share * (1 - low), share)].astype(jnp.bfloat16)
         across[piece] = copies.start(zsend.at[piece], zrecv.at[piece], near)
 
@@ -787,6 +855,20 @@
         zkeep[piece] = own + zrecv[piece].astype(jnp.float32)
 
     def send_far(chunk):
+        if chunk == final:
+            for side in range(2):
+                for half_side in range(2):
+                    part = acc[2 * chunk + side, 0, pl.ds(share * half_side, share)]
+                    lsend[2 * side + half_side] = part.astype(jnp.bfloat16)
+            over[chunk] = [
+                copies.start(
+                    lsend.at[(here + step) % groups],
+                    lrecv.at[step - 1],
+                    {"vars": (here + step) % groups},
+                )
+                for step in range(1, groups)
+            ]
+            return
         for side in range(2):
             sum_near(2 * chunk + side)
         ysend[chunk] = zkeep[2 * chunk + 1 - top].astype(jnp.bfloat16)
@@ -797,6 +879,19 @@
         return total.at[chunk, which, pl.ds(0, count_back)]
 
     def sum_far(chunk):
+        if chunk == final:
+            value = acc[2 * chunk + top, 0, pl.ds(share * low, share)]
+            for step, copy in enumerate(over[chunk]):
+                copy.wait_recv()
+                value = value + lrecv[step].astype(jnp.float32)
+            total[chunk, here] = value.astype(jnp.bfloat16)
+            around[chunk] = [
+                copies.start(
+                    quarter(chunk, here), quarter(chunk, here), {"vars": (here + step) % groups}
+                )
+                for step in range(1, groups)
+            ]
+            return
         over[chunk].wait_recv()
         value = zkeep[2 * chunk + top] + yrecv[chunk].astype(jnp.float32)
         total[chunk, here] = value.astype(jnp.bfloat16)
@@ -807,11 +902,17 @@
         ]
 
     def pass_on(chunk):
+        if chunk == final:
+            return
         around[chunk][0].wait_recv()
         other_quarter = quarter(chunk, (here + 2) % groups)
         forward[chunk] = copies.start(other_quarter, other_quarter, near)
 
     def finish(chunk):
+        if chunk == final:
+            for copy in around[chunk]:
+                copy.wait_recv()
+            return
         around[chunk][1].wait_recv()
         forward[chunk].wait_recv()
 
@@ -827,12 +928,12 @@
     stages += [pieces(send_near), send_far, sum_far, pass_on, finish]
     extra = {1: [vec_begin], len(stages) - 3: [slots.begin]}
     for level in range(bits):
-        tick = min(3 + 2 * level, CHUNKS + len(stages) - 2)
+        tick = min(4 + 2 * level, CHUNKS + len(stages) - 2)
         extra.setdefault(tick, []).append(functools.partial(vecs.advance, level))
         tick = min(len(stages) - 1 + level, CHUNKS + len(stages) - 2)
         extra.setdefault(tick, []).append(functools.partial(slots.advance, level))
     for tick in range(CHUNKS + len(stages) - 1):
-        for stage in reversed(range(len(stages))):
+        for stage in range(len(stages)):
             place = tick - stage
             if 0 <= place < CHUNKS:
                 stages[stage](ORDER[place])
@@ -850,7 +951,8 @@
     half = CHUNK // 2
     pieces = 2 * CHUNKS
     share = CHUNK // groups
-    copies = 2 * (groups - 1) + pieces * (bits + 1) + 4 * CHUNKS + 2 + 2 * (count - 1)
+    copies = 4 * (groups - 1) + (pieces - 2) * (bits + 1) + 2 * bits
+    copies += 4 * (CHUNKS - 1) + 2 + 2 * (count - 1)
     bfloat = jnp.bfloat16
     vmem = pl.BlockSpec(memory_space=pltpu.VMEM)
     return pl.pallas_call(
@@ -861,7 +963,7 @@
             jax.ShapeDtypeStruct((count, groups) + vec.shape, jnp.float32),
             jax.ShapeDtypeStruct(field.shape, field.dtype),
         ),
-        in_specs=[vmem] * 4,
+        in_specs=[pl.BlockSpec(memory_space=pl.ANY)] + [vmem] * 3,
         out_specs=(vmem,) * 4,
         scratch_shapes=[
             pltpu.VMEM((pieces, half, count // 2, rows, WIDTH), bfloat),
@@ -873,6 +975,10 @@
             pltpu.VMEM((pieces, share, rows, WIDTH), jnp.float32),
             pltpu.VMEM((CHUNKS, share, rows, WIDTH), bfloat),
             pltpu.VMEM((CHUNKS, share, rows, WIDTH), bfloat),
+            pltpu.VMEM((groups, share, rows, WIDTH), bfloat),
+            pltpu.VMEM((groups - 1, share, rows, WIDTH), bfloat),
+            pltpu.VMEM((CHUNKS * CHUNK - groups, count // 2, rows, WIDTH), bfloat),
+            pltpu.SemaphoreType.DMA((1,)),
             pltpu.SemaphoreType.DMA((copies,)),
             pltpu.SemaphoreType.DMA((copies,)),
         ],
@@ -894,14 +1000,19 @@
         out[at] = value
 
 
-def update_kernel(groups, sum_ref, slot_ref, vec_ref, *refs):
+def update_kernel(groups, sum_ref, slot_ref, vec_ref, back_ref, *refs):
     flt = jnp.float32
     slot_in, square_in, wide_in, mlp_in, vector_in = (refs[3 * i : 3 * i + 3] for i in range(5))
     refs = refs[15:]
+    field_out = refs[-1]
     slot_out, square_out, wide_out, mlp_out, vector_out = (
         refs[4 * i : 4 * i + 4] for i in range(5)
     )
     own = wide_in[0].shape[0]
+    for group in range(groups):
+        rows = back_ref[group].astype(flt)
+        for slot in range(field_out.shape[0]):
+            field_out[slot, group] = rows[slot * PATCH : (slot + 1) * PATCH]
     bfloat = jnp.bfloat16
     last = CHUNKS - 1
 
@@ -960,25 +1071,27 @@
         renew_into(slot_out, slot_in, (p,), jnp.concatenate(pieces, axis=1), EMBED_RATE)
 
 
-def update_all(groups, sums, slot_blocks, vec_all, parameters):
+def update_all(groups, sums, slot_blocks, vec_all, field_back, parameters):
     vmem = pl.BlockSpec(memory_space=pltpu.VMEM)
     shapes = [jax.ShapeDtypeStruct(a.shape, a.dtype) for a in parameters[::3] for _ in range(4)]
+    field_shape = (parameters[0].shape[1], groups, PATCH, field_back.shape[2])
+    shapes.append(jax.ShapeDtypeStruct(field_shape, jnp.float32))
     return pl.pallas_call(
         functools.partial(update_kernel, groups),
         out_shape=tuple(shapes),
-        in_specs=[vmem] * (3 + len(parameters)),
+        in_specs=[vmem] * (4 + len(parameters)),
         out_specs=(vmem,) * len(shapes),
         compiler_params=pltpu.CompilerParams(vmem_limit_bytes=60 << 20),
-    )(sums, slot_blocks, vec_all, *parameters)
+    )(sums, slot_blocks, vec_all, field_back, *parameters)
 
 
 def gather_kernel(
     count,
     groups,
+    ids_ref,
     field_ref,
     slot_ref,
-    ident_ref,
-    cond_ref,
+    cond_in,
     square_ref,
     wide_ref,
     mlp_ref,
@@ -991,11 +1104,16 @@
     qkv_out,
     mlp_out,
     field_all,
+    slot_src,
     slot_all,
-    ident_all,
+    cond_ref,
     cond_all,
     part,
     part_in,
+    square_own,
+    qkv_own,
+    mlp_own,
+    own_sem,
     send_sem,
     recv_sem,
 ):
@@ -1004,16 +1122,37 @@
     dp, here = lax.axis_index("dp"), lax.axis_index("vars")
     own, rows = square_ref.shape[1], square_out.shape[2]
     if own < rows:
-        square_out[:, dp] = jnp.zeros_like(square_out[:, dp])
-        qkv_out[dp] = jnp.zeros_like(qkv_out[dp])
-        mlp_out[:, dp] = jnp.zeros_like(mlp_out[:, dp])
-    square_out[:, dp, :own] = square_ref[...].astype(bfloat)
-    qkv_out[dp, :own] = wide_ref[:, : 3 * D].astype(bfloat)
-    mlp_out[:, dp, :own] = mlp_ref[...].astype(bfloat)
+        for ref in (square_own, qkv_own, mlp_own):
+            ref[...] = jnp.zeros_like(ref)
+    square_own[:, :own] = square_ref[...].astype(bfloat)
+    qkv_own[:own] = wide_ref[:, : 3 * D].astype(bfloat)
+    mlp_own[:, :own] = mlp_ref[...].astype(bfloat)
+    kept = [
+        pltpu.make_async_copy(square_own, square_out.at[:, dp], own_sem.at[0]),
+        pltpu.make_async_copy(qkv_own, qkv_out.at[dp], own_sem.at[1]),
+        pltpu.make_async_copy(mlp_own, mlp_out.at[:, dp], own_sem.at[2]),
+    ]
+    for copy in kept:
+        copy.start()
+    raw = cond_in[...].astype(flt)
+    cond = (raw * jax.nn.sigmoid(raw)).astype(bfloat).astype(flt)
+    cond_ref[...] = jnp.broadcast_to(cond, cond_ref.shape)
     cond_all[dp] = cond_ref[...]
+    each = slot_ref.shape[1]
+    per = slot_src.shape[1]
+    pieces = 3 * (PATCH + 1)
+    for piece in range(count * per):
+        block, at = piece // per, piece % per
+        if piece < pieces:
+            lane = piece % 3 * WIDTH
+            slot_src[block, at] = slot_ref[piece // 3, :, lane : lane + WIDTH]
+        else:
+            slot_src[block, at] = jnp.zeros((each, WIDTH), flt)
+    for row in range(each):
+        ident = jnp.full((1, WIDTH), ids_ref[0, row], jnp.int32).astype(flt)
+        slot_src[pieces // per, pieces % per, row : row + 1] = ident
     greet(dp, here, range(1, count), bits, groups)
     copies = Copies(send_sem, recv_sem)
-    most = PATCH // 2 + 1
     forth = list(range(1, bits)) + [0]
     back = list(range(1, bits))[::-1] + [0]
     ones = Spread(
@@ -1022,27 +1161,31 @@
         dp,
         bits,
         forth,
-    )
-    twos = Spread(copies, [lambda block: mlp_out.at[:, block]], dp, bits, back)
+        [square_own, qkv_own],
+    )
+    twos = Spread(copies, [lambda block: mlp_out.at[:, block]], dp, bits, back, [mlp_own])
     conds = [
         copies.start(cond_ref, cond_all.at[dp], {"dp": (dp + step) % count})
         for step in range(1, count)
     ]
-    core = dp % 2
-    arrivals, slot_copies = [], []
-    sent = pl.ds(core * (PATCH + 1 - most), most)
-    for step in range(1, groups):
-        to = {"vars": (here + step) % groups}
-        arrivals.append(copies.start(ident_ref, ident_all.at[here], to))
-        slot_copies.append(copies.start(slot_ref.at[sent], slot_all.at[here, sent], to))
+    arrivals = []
+    slot_copies = [
+        copies.start(
+            slot_src.at[dp], slot_all.at[dp, here], {"vars": (here + step) % groups}
+        )
+        for step in range(1, groups)
+    ]
+    trees = [
+        Spread(copies, [lambda block, at=at: slot_all.at[block, :, at]], dp, bits, order)
+        for at, order in zip(range(per), (forth, back))
+    ]
     ones.begin()
     twos.begin()
     for step in range(1, groups):
         to = (here + step) % groups
         arrivals.append(copies.start(field_ref.at[to], field_all.at[here], {"vars": to}))
     field_all[here] = field_ref[here]
-    slot_all[here] = slot_ref[...]
-    ident_all[here] = ident_ref[...]
+    slot_all[dp, here] = slot_src[dp]
     for copy in conds:
         copy.wait_recv()
     cond = cond_all[:, 0, :].astype(bfloat)
@@ -1061,17 +1204,12 @@
         copies.start(part.at[(dp + step) % count], part_in.at[step - 1], {"dp": (dp + step) % count})
         for step in range(1, count)
     ]
-    ones.advance(0)
-    twos.advance(0)
-    fewer = PATCH + 1 - most
-    given = pl.ds(core * most, fewer)
-    for step, copy in enumerate(slot_copies, 1):
+    for copy in slot_copies:
         copy.wait_recv()
-        block = slot_all.at[(here - step + groups) % groups, given]
-        arrivals.append(copies.start(block, block, {"dp": dp + 1 - 2 * core}))
-    for level in range(1, bits):
-        ones.advance(level)
-        twos.advance(level)
+    for tree in trees:
+        tree.begin()
+    for stream in (ones, twos, *trees):
+        stream.advance(0)
     for copy in part_copies:
         copy.wait_recv()
     mine = part[dp]
@@ -1093,32 +1231,43 @@
         axis=0,
     )
     cols_out[...] = columns.T
+    for level in range(1, bits - 1):
+        for stream in (*trees, ones, twos):
+            stream.advance(level)
+    for tree in trees:
+        tree.advance(bits - 1)
+    spare = SLOT_ROWS - groups * each
+    def slot_piece(piece, fill):
+        rows = [slot_all[piece // per, source, piece % per] for source in range(groups)]
+        rows.append(jnp.full((spare, WIDTH), fill, flt))
+        return jnp.concatenate(rows, axis=0)
+
+    for piece in range(pieces):
+        base, lane = piece // 3 * SLOT_ROWS, piece % 3 * WIDTH
+        slots_out[base : base + SLOT_ROWS, lane : lane + WIDTH] = slot_piece(piece, 0.0)
+    mask_out[...] = jnp.where(slot_piece(pieces, float(NVARS)) < NVARS, 0.0, FAR)
     for copy in arrivals:
         copy.wait_recv()
-    each = slot_ref.shape[1]
-    spare = SLOT_ROWS - groups * each
     for p in range(PATCH):
-        pieces = [
+        rows = [
             field_all[source, p * each : (p + 1) * each].astype(flt) for source in range(groups)
         ]
-        pieces.append(jnp.zeros((spare, field_ref.shape[2]), flt))
-        patch_out[p] = jnp.concatenate(pieces, axis=0).astype(bfloat)
-    for p in range(PATCH + 1):
-        pieces = [slot_all[source, p] for source in range(groups)]
-        pieces.append(jnp.zeros((spare, D), flt))
-        slots_out[p * SLOT_ROWS : (p + 1) * SLOT_ROWS] = jnp.concatenate(pieces, axis=0)
-    pieces = [ident_all[source, :each] for source in range(groups)]
-    pieces.append(jnp.full((spare, WIDTH), float(NVARS), flt))
-    mask_out[...] = jnp.where(jnp.concatenate(pieces, axis=0) < NVARS, 0.0, FAR)
+        rows.append(jnp.zeros((spare, field_ref.shape[2]), flt))
+        patch_out[p] = jnp.concatenate(rows, axis=0).astype(bfloat)
+    for stream in (ones, twos):
+        stream.advance(bits - 1)
+    for copy in kept:
+        copy.wait()
     copies.finish()
 
 
-def gather_all(count, groups, field, slots, ident, cond, square, wide, mlp, vectors):
+def gather_all(count, groups, ids, field, slots, cond, square, wide, mlp, vectors):
     bits = count.bit_length() - 1
     own = square.shape[1]
     rows = -(-own // 16) * 16
     bfloat, flt = jnp.bfloat16, jnp.float32
-    copies = 4 * (groups - 1) + 5 * (count - 1)
+    per = -(-(3 * (PATCH + 1) + 1) // count)
+    copies = 2 * (groups - 1) + (5 + min(per, 2)) * (count - 1)
     length = field.shape[2]
     strips = (wide.shape[1] - 3 * D) // WIDTH
     vmem = pl.BlockSpec(memory_space=pltpu.VMEM)
@@ -1134,22 +1283,27 @@
     return pl.pallas_call(
         functools.partial(gather_kernel, count, groups),
         out_shape=tuple(jax.ShapeDtypeStruct(shape, dtype) for shape, dtype in outs),
-        in_specs=[vmem] * 8,
-        out_specs=(vmem,) * len(outs),
+        in_specs=[pl.BlockSpec(memory_space=pltpu.SMEM)] + [vmem] * 7,
+        out_specs=(vmem,) * 4 + (pl.BlockSpec(memory_space=pl.ANY),) * 3,
         scratch_shapes=[
             pltpu.VMEM((groups,) + field.shape[1:], bfloat),
-            pltpu.VMEM((groups,) + slots.shape, flt),
-            pltpu.VMEM((groups,) + ident.shape, flt),
+            pltpu.VMEM((count, per, slots.shape[1], WIDTH), flt),
+            pltpu.VMEM((count, groups, per, slots.shape[1], WIDTH), flt),
+            pltpu.VMEM((8, D), flt),
             pltpu.VMEM((count, 8, D), flt),
             pltpu.VMEM((count, strips, WIDTH), flt),
             pltpu.VMEM((count - 1, strips, WIDTH), flt),
+            pltpu.VMEM((4, rows, D), bfloat),
+            pltpu.VMEM((rows, 3 * D), bfloat),
+            pltpu.VMEM((2, rows, 4 * D), bfloat),
+            pltpu.SemaphoreType.DMA((3,)),
             pltpu.SemaphoreType.DMA((copies,)),
             pltpu.SemaphoreType.DMA((copies,)),
         ],
         compiler_params=pltpu.CompilerParams(
             collective_id=1, has_side_effects=True, vmem_limit_bytes=60 << 20
         ),
-    )(field, slots, ident, cond, square, wide, mlp, vectors)
+    )(ids, field, slots, cond, square, wide, mlp, vectors)
 
 
 def on_device(
@@ -1179,17 +1333,15 @@
     count, groups = lax.axis_size("dp"), lax.axis_size("vars")
     own = square.shape[1]
     rows = -(-own // 16) * 16
-    cond_low = jax.nn.silu(condition[0].astype(jnp.float32)).astype(bfloat).astype(jnp.float32)
     field = jnp.transpose(fields[:, 0], (1, 2, 0, 3)).reshape(groups, -1, length)
     field = jnp.pad(field, ((0, 0), (0, -field.shape[1] % 16), (0, 0)))
-    ident = jnp.broadcast_to(var_ids.astype(jnp.float32)[:, None], (slot_weights.shape[0], WIDTH))
     gathered = gather_all(
         count,
         groups,
+        var_ids[None],
         field,
         jnp.transpose(slot_weights, (1, 0, 2)),
-        ident,
-        jnp.broadcast_to(cond_low, (8, D)),
+        condition[0],
         square,
         wide,
         mlp,
@@ -1220,6 +1372,7 @@
         sums,
         slot_blocks,
         vec_all.reshape(-1, VEC_ROWS, D),
+        field_back,
         (
             *(jnp.transpose(a, (1, 0, 2)) for a in (slot_weights, slot_momentum, slot_average)),
             square,
@@ -1236,11 +1389,9 @@
             vectors_average,
         ),
     )
-    each = slot_weights.shape[0]
-    field_back = field_back[:, : PATCH * each].reshape(groups, PATCH, each, length)
-    field_grad = jnp.transpose(field_back, (2, 0, 1, 3)).astype(jnp.float32)[:, None]
+    field_grad = updated[-1][:, None]
     slot_new = tuple(jnp.transpose(a, (1, 0, 2)) for a in updated[:4])
-    return (block_out[None, None], field_grad) + slot_new + tuple(updated[4:])
+    return (block_out[None, None], field_grad) + slot_new + tuple(updated[4:-1])
 
 
 def solution(mesh):

time: 188 us -> 166 us (0.88)
  Pallas kernels: 177 us -> 162 us
  local copies, waits for them, and re-layouts: 6.35 us -> 2.45 us
  other arithmetic: 2.56 us -> 0 us
    pallas_call x1, Pallas kernels: 78.8 us -> 59.6 us  [block_step(): pl.pallas_call(functools.partial(block_kernel, groups * count * length, g...]
    broadcast_in_dim x3 -> x0, local copies, waits for them, and re-layouts: 2.04 us -> none  [the longest x1 0.76 us: on_device(): jnp.transpose(field_back, (2, 0, 1, 3)).astype(jnp.float32)[:, None]]
where the time goes in v1:
time: 166 us; the launch traced here: 165 us
  Pallas kernels  162 us (98%)
  local copies, waits for them, and re-layouts  2.45 us (1%)
    pallas_call x1, Pallas kernels, block_step(): pl.pallas_call(functools.partial(block_kernel, groups * count * length, g...  59.6 us
    pallas_call x1, Pallas kernels, reduce_all(): pl.pallas_call(functools.partial(reduce_kernel, count, groups), out_shape...  57.9 us
    pallas_call x1, Pallas kernels, gather_all(): pl.pallas_call(functools.partial(gather_kernel, count, groups), out_shape...  36.1 us
    pallas_call x1, Pallas kernels, update_all(): pl.pallas_call(functools.partial(update_kernel, groups), out_shape=tuple(...  7.98 us

profile of v1, /device:TPU:0, one launch (start us, length us, event | category | flops | bytes accessed | tf_op | source)
XLA Modules:
  0.0 164.9 jit_solution(6697657769643384520)
XLA Ops:
  0.7 1.4 copy.44
  2.0 0.2 copy.45
  2.2 0.9 pad.4.field_ref
  3.1 36.1 %shard_map.363 = (bf16[4,80,1024]{2,1,0:T(8,128)(2,1)}, f32[400,384]{1,0:T(8,128)}, f32[80,128]{1,0:T(8,128)}, f32[384,128]{1,0:T(8,128)}, bf16[4,8,48,384]{3,2,...) custom-call(s32[1,18]{1,0:T(1,128)} %bitcast.39, bf16[4,80,1024]{2,1,0:T(8,128)(2,1)} %pad.4.field_ref, ...), custom_call_target="tpu_custom_call" | custom-call | tf_op jit(solution)/shard_map/pallas_call | solution.py:1283
  39.2 59.6 %shard_map.364 = (bf16[1024,384]{1,0:T(8,128)(2,1)}, bf16[44,384,128]{2,1,0:T(8,128)(2,1)}, bf16[4,4,2,48,128]{4,3,2,1,0:T(8,128)(2,1)}, f32[16,384]{1,0:T(8,128)}, bf16[4,80,1024]{2,1,0:T(8,128)(2,1)}) custom-call(s32[1,1024]{1,0:T(1,128)} %bitcast.36, bf16[4,80,1024]{2,1,0:T(8,128)(2,1)} %get-tuple-element.59.fields_ref, ...), custom_call_target="tpu_custom_call" | custom-call | tf_op jit(solution)/shard_map/pallas_call | solution.py:586
  98.9 57.9 %shard_map.365 = (bf16[4,4,3,48,128]{4,3,2,1,0:T(8,128)(2,1)}, f32[8,48,128]{2,1,0:T(8,128)}, f32[8,4,16,384]{3,2,1,0:T(8,128)}, bf16[4,80,1024]{2,1,0:T(8,128)(2,1)}) custom-call(bf16[44,4,2,48,128]{4,3,2,1,0:T(8,128)(2,1)} %bitcast.24, bf16[4,4,2,48,128]{4,3,2,1,0:T(8,128)(2,1)} %get-tuple-element.68.s_ref, f32[16,384]{1,0:T(8,128)} %get-tuple-element.69.vec_ref, ...), custom_call_target="tpu_custom_call" | custom-call | tf_op jit(solution)/shard_map/pallas_call | solution.py:958
  156.7 8.0 %shard_map.366 = (f32[5,18,384]{2,1,0:T(8,128)}, f32[5,18,384]{2,1,0:T(8,128)}, f32[5,18,384]{2,1,0:T(8,128)}, f32[5,18,384]{2,1,0:T(8,128)}, f32[4,48,384]{2,1,...) custom-call(bf16[4,4,3,48,128]{4,3,2,1,0:T(8,128)(2,1)} %get-tuple-e, ...), custom_call_target="tpu_custom_call" | custom-call | tf_op jit(solution)/shard_map/pallas_call | solution.py:1079

commit v2 on v1

--- a/solution.py
+++ b/solution.py
@@ -336,11 +336,17 @@
         grad_branch[:, at] = low_grad
         column_acc[3] += fold(low_grad.astype(flt))
         grad_in = jnp.zeros((depth, TILE), flt)
-        for block in range(HEADS):
-            part = slice(block * TILE, (block + 1) * TILE)
-            ups = (matmul(down_t[part], low_grad) * raw[block // team_size, block % team_size]).astype(bfloat)
-            grad_up[part, at] = ups
-            grad_in = grad_in + matmul(mlp_ref[0, :, part], ups)
+        for base in range(0, HEADS, 3):
+            blocks = range(base, base + 3)
+            backs = [matmul(down_t[b * TILE : (b + 1) * TILE], low_grad) for b in blocks]
+            lows = []
+            for block, back in zip(blocks, backs):
+                ups = (back * raw[block // team_size, block % team_size]).astype(bfloat)
+                grad_up[block * TILE : (block + 1) * TILE, at] = ups
+                lows.append(ups)
+            for block, ups in zip(blocks, lows):
+                part = slice(block * TILE, (block + 1) * TILE)
+                grad_in = grad_in + matmul(mlp_ref[0, :, part], ups)
         column_acc[8] += fold(grad_in * normed)
         column_acc[7] += fold(grad_in)
         grad = grad + normalize_cols_back(grad_in * (1.0 + column(8)), normed, inv)
@@ -708,7 +714,8 @@
     field_ref,
     total,
     slot_ref,
-    vec_all,
+    ada_ref,
+    sums_ref,
     field_out,
     recv0,
     acc,
@@ -721,6 +728,7 @@
     yrecv,
     lsend,
     lrecv,
+    vec_all,
     g_own,
     own_sem,
     send_sem,
@@ -782,6 +790,24 @@
     vecs = Spread(copies, [lambda block: vec_all.at[block]], dp, bits, forth)
     slots = Spread(copies, [lambda block: slot_ref.at[block]], dp, bits, forth)
 
+    def vec_finish():
+        own = ada_ref.shape[0]
+        sums = vec_all[0, 0]
+        for device in range(1, count * groups):
+            sums = sums + vec_all[device // groups, device % groups]
+        sums_ref[...] = sums
+        device_rows = vec_all[...].reshape(count * groups, VEC_ROWS, D)
+        pick = lax.broadcasted_iota(jnp.int32, (D, own), 0) == dp * own + lax.broadcasted_iota(
+            jnp.int32, (D, own), 1
+        )
+        pick = jnp.where(pick, 1.0, 0.0).astype(jnp.bfloat16)
+        conditions = matmul(device_rows[:, 11, :].astype(jnp.bfloat16), pick)
+        conditions = conditions.T.astype(jnp.bfloat16)
+        for row in range(6):
+            upper, rest = halves(device_rows[:, 5 + row, :])
+            grads = matmul(conditions, upper) + matmul(conditions, rest)
+            ada_ref[:, row * D : (row + 1) * D] = grads
+
     def vec_begin():
         for copy in vec_copies:
             copy.wait_recv()
@@ -932,6 +958,7 @@
         extra.setdefault(tick, []).append(functools.partial(vecs.advance, level))
         tick = min(len(stages) - 1 + level, CHUNKS + len(stages) - 2)
         extra.setdefault(tick, []).append(functools.partial(slots.advance, level))
+    extra.setdefault(min(4 + 2 * bits - 2, CHUNKS + len(stages) - 2), []).append(vec_finish)
     for tick in range(CHUNKS + len(stages) - 1):
         for stage in range(len(stages)):
             place = tick - stage
@@ -960,11 +987,12 @@
         out_shape=(
             jax.ShapeDtypeStruct((CHUNKS, groups, share, rows, WIDTH), bfloat),
             jax.ShapeDtypeStruct((count, rows, WIDTH), jnp.float32),
-            jax.ShapeDtypeStruct((count, groups) + vec.shape, jnp.float32),
+            jax.ShapeDtypeStruct((D // count, 6 * D), jnp.float32),
+            jax.ShapeDtypeStruct(vec.shape, jnp.float32),
             jax.ShapeDtypeStruct(field.shape, field.dtype),
         ),
         in_specs=[pl.BlockSpec(memory_space=pl.ANY)] + [vmem] * 3,
-        out_specs=(vmem,) * 4,
+        out_specs=(vmem,) * 5,
         scratch_shapes=[
             pltpu.VMEM((pieces, half, count // 2, rows, WIDTH), bfloat),
             pltpu.VMEM((pieces, count // 4, half, rows, WIDTH), jnp.float32),
@@ -977,6 +1005,7 @@
             pltpu.VMEM((CHUNKS, share, rows, WIDTH), bfloat),
             pltpu.VMEM((groups, share, rows, WIDTH), bfloat),
             pltpu.VMEM((groups - 1, share, rows, WIDTH), bfloat),
+            pltpu.VMEM((count, groups) + vec.shape, jnp.float32),
             pltpu.VMEM((CHUNKS * CHUNK - groups, count // 2, rows, WIDTH), bfloat),
             pltpu.SemaphoreType.DMA((1,)),
             pltpu.SemaphoreType.DMA((copies,)),
@@ -1000,7 +1029,7 @@
         out[at] = value
 
 
-def update_kernel(groups, sum_ref, slot_ref, vec_ref, back_ref, *refs):
+def update_kernel(groups, sum_ref, slot_ref, ada_ref, vec_ref, back_ref, *refs):
     flt = jnp.float32
     slot_in, square_in, wide_in, mlp_in, vector_in = (refs[3 * i : 3 * i + 3] for i in range(5))
     refs = refs[15:]
@@ -1044,21 +1073,9 @@
     renew_into(
         square_out, square_in, (0,), matmul(keys, asked_high) + matmul(keys, asked_low), RATE
     )
-    devices = vec_ref.shape[0]
-    pick = lax.broadcasted_iota(jnp.int32, (D, own), 0) == lax.axis_index(
-        "dp"
-    ) * own + lax.broadcasted_iota(jnp.int32, (D, own), 1)
-    conditions = matmul(vec_ref[:, 11, :].astype(bfloat), jnp.where(pick, 1.0, 0.0).astype(bfloat))
-    conditions = conditions.T.astype(bfloat)
-    for row in range(6):
-        high, low = halves(vec_ref[:, 5 + row, :])
-        part = (slice(None), slice((3 + row) * D, (4 + row) * D))
-        grads = matmul(conditions, high) + matmul(conditions, low)
-        renew_into(wide_out, wide_in, part, grads, RATE)
-    total = vec_ref[0]
-    for device in range(1, devices):
-        total = total + vec_ref[device]
-    renew_into(vector_out, vector_in, (slice(None),), total[:11], RATE)
+    part = (slice(None), slice(3 * D, 9 * D))
+    renew_into(wide_out, wide_in, part, ada_ref[...], RATE)
+    renew_into(vector_out, vector_in, (slice(None),), vec_ref[:11], RATE)
     each = slot_in[0].shape[1]
     blocks = slot_ref.shape[0]
     size = slot_share((PATCH + 1) * each, blocks)
@@ -1071,7 +1088,7 @@
         renew_into(slot_out, slot_in, (p,), jnp.concatenate(pieces, axis=1), EMBED_RATE)
 
 
-def update_all(groups, sums, slot_blocks, vec_all, field_back, parameters):
+def update_all(groups, sums, slot_blocks, ada, vec_sums, field_back, parameters):
     vmem = pl.BlockSpec(memory_space=pltpu.VMEM)
     shapes = [jax.ShapeDtypeStruct(a.shape, a.dtype) for a in parameters[::3] for _ in range(4)]
     field_shape = (parameters[0].shape[1], groups, PATCH, field_back.shape[2])
@@ -1079,10 +1096,10 @@
     return pl.pallas_call(
         functools.partial(update_kernel, groups),
         out_shape=tuple(shapes),
-        in_specs=[vmem] * (4 + len(parameters)),
+        in_specs=[vmem] * (5 + len(parameters)),
         out_specs=(vmem,) * len(shapes),
         compiler_params=pltpu.CompilerParams(vmem_limit_bytes=60 << 20),
-    )(sums, slot_blocks, vec_all, field_back, *parameters)
+    )(sums, slot_blocks, ada, vec_sums, field_back, *parameters)
 
 
 def gather_kernel(
@@ -1103,6 +1120,7 @@
     square_out,
     qkv_out,
     mlp_out,
+    field_src,
     field_all,
     slot_src,
     slot_all,
@@ -1134,6 +1152,12 @@
     ]
     for copy in kept:
         copy.start()
+    used, packed = field_ref.shape[1], field_src.shape[1]
+    for group in range(groups):
+        pieces = [field_ref[group].astype(flt)]
+        if packed > used:
+            pieces.append(jnp.zeros((packed - used, field_ref.shape[2]), flt))
+        field_src[group] = jnp.concatenate(pieces, axis=0).astype(bfloat)
     raw = cond_in[...].astype(flt)
     cond = (raw * jax.nn.sigmoid(raw)).astype(bfloat).astype(flt)
     cond_ref[...] = jnp.broadcast_to(cond, cond_ref.shape)
@@ -1183,8 +1207,8 @@
     twos.begin()
     for step in range(1, groups):
         to = (here + step) % groups
-        arrivals.append(copies.start(field_ref.at[to], field_all.at[here], {"vars": to}))
-    field_all[here] = field_ref[here]
+        arrivals.append(copies.start(field_src.at[to], field_all.at[here], {"vars": to}))
+    field_all[here] = field_src[here]
     slot_all[dp, here] = slot_src[dp]
     for copy in conds:
         copy.wait_recv()
@@ -1269,6 +1293,7 @@
     per = -(-(3 * (PATCH + 1) + 1) // count)
     copies = 2 * (groups - 1) + (5 + min(per, 2)) * (count - 1)
     length = field.shape[2]
+    packed = -(-field.shape[1] // 16) * 16
     strips = (wide.shape[1] - 3 * D) // WIDTH
     vmem = pl.BlockSpec(memory_space=pltpu.VMEM)
     outs = [
@@ -1286,7 +1311,8 @@
         in_specs=[pl.BlockSpec(memory_space=pltpu.SMEM)] + [vmem] * 7,
         out_specs=(vmem,) * 4 + (pl.BlockSpec(memory_space=pl.ANY),) * 3,
         scratch_shapes=[
-            pltpu.VMEM((groups,) + field.shape[1:], bfloat),
+            pltpu.VMEM((groups, packed, length), bfloat),
+            pltpu.VMEM((groups, packed, length), bfloat),
             pltpu.VMEM((count, per, slots.shape[1], WIDTH), flt),
             pltpu.VMEM((count, groups, per, slots.shape[1], WIDTH), flt),
             pltpu.VMEM((8, D), flt),
@@ -1334,7 +1360,6 @@
     own = square.shape[1]
     rows = -(-own // 16) * 16
     field = jnp.transpose(fields[:, 0], (1, 2, 0, 3)).reshape(groups, -1, length)
-    field = jnp.pad(field, ((0, 0), (0, -field.shape[1] % 16), (0, 0)))
     gathered = gather_all(
         count,
         groups,
@@ -1364,14 +1389,15 @@
         columns,
         cotangent[0, 0],
     )
-    sums, slot_blocks, vec_all, field_back = reduce_all(
+    sums, slot_blocks, ada, vec_sums, field_back = reduce_all(
         count, groups, pack_rows(grads, count, rows), slots_packed, vec, field
     )
     updated = update_all(
         groups,
         sums,
         slot_blocks,
-        vec_all.reshape(-1, VEC_ROWS, D),
+        ada,
+        vec_sums,
         field_back,
         (
             *(jnp.transpose(a, (1, 0, 2)) for a in (slot_weights, slot_momentum, slot_average)),

time: 166 us -> 164 us (0.988)
  Pallas kernels: 162 us -> 160 us
    pallas_call x1, Pallas kernels: 57.9 us -> 49.8 us  [reduce_all(): pl.pallas_call(functools.partial(reduce_kernel, count, groups), out_shape...]
    pallas_call x1, Pallas kernels: 59.6 us -> 67 us  [block_step(): pl.pallas_call(functools.partial(block_kernel, groups * count * length, g...]
where the time goes in v2:
time: 164 us; the launch traced here: 163 us
  Pallas kernels  160 us (98%)
  local copies, waits for them, and re-layouts  2.36 us (1%)
    pallas_call x1, Pallas kernels, block_step(): pl.pallas_call(functools.partial(block_kernel, groups * count * length, g...  67 us
    pallas_call x1, Pallas kernels, reduce_all(): pl.pallas_call(functools.partial(reduce_kernel, count, groups), out_shape...  49.8 us
    pallas_call x1, Pallas kernels, gather_all(): pl.pallas_call(functools.partial(gather_kernel, count, groups), out_shape...  36.1 us
    pallas_call x1, Pallas kernels, update_all(): pl.pallas_call(functools.partial(update_kernel, groups), out_shape=tuple(...  6.93 us

profile of v2, /device:TPU:0, one launch (start us, length us, event | category | flops | bytes accessed | tf_op | source)
XLA Modules:
  0.0 163.1 jit_solution(5152936947231033880)
XLA Ops:
  0.7 1.4 copy.44
  2.0 1.0 copy.45.field_ref
  3.0 36.1 %shard_map.363 = (bf16[4,80,1024]{2,1,0:T(8,128)(2,1)}, f32[400,384]{1,0:T(8,128)}, f32[80,128]{1,0:T(8,128)}, f32[384,128]{1,0:T(8,128)}, bf16[4,8,48,384]{3,2,...) custom-call(s32[1,18]{1,0:T(1,128)} %bitcast.37, bf16[4,72,1024]{2,1,0:T(8,128)(2,1)} %copy.45.field_ref, ...), custom_call_target="tpu_custom_call" | custom-call | tf_op jit(solution)/shard_map/pallas_call | solution.py:1308
  39.1 67.0 %shard_map.364 = (bf16[1024,384]{1,0:T(8,128)(2,1)}, bf16[44,384,128]{2,1,0:T(8,128)(2,1)}, bf16[4,4,2,48,128]{4,3,2,1,0:T(8,128)(2,1)}, f32[16,384]{1,0:T(8,128)}, bf16[4,80,1024]{2,1,0:T(8,128)(2,1)}) custom-call(s32[1,1024]{1,0:T(1,128)} %bitcast.34, bf16[4,80,1024]{2,1,0:T(8,128)(2,1)} %get-tuple-element.60.fields_ref, ...), custom_call_target="tpu_custom_call" | custom-call | tf_op jit(solution)/shard_map/pallas_call | solution.py:592
  106.2 49.8 %shard_map.365 = (bf16[4,4,3,48,128]{4,3,2,1,0:T(8,128)(2,1)}, f32[8,48,128]{2,1,0:T(8,128)}, f32[48,2304]{1,0:T(8,128)}, f32[16,384]{1,0:T(8,128)}, bf16[4,80,1024]{2,1,0:T(8,128)(2,1)}) custom-call(bf16[44,4,2,48,128]{4,3,2,1,0:T(8,128)(2,1)} %bitcast.23, bf16[4,4,2,48,128]{4,3,2,1,0:T(8,128)(2,1)} %get-tuple-element.69.s_ref, ...), custom_call_target="tpu_custom_call" | custom-call | tf_op jit(solution)/shard_map/pallas_call | solution.py:985
  156.0 6.9 %shard_map.366 = (f32[5,18,384]{2,1,0:T(8,128)}, f32[5,18,384]{2,1,0:T(8,128)}, f32[5,18,384]{2,1,0:T(8,128)}, f32[5,18,384]{2,1,0:T(8,128)}, f32[4,48,384]{2,1,...) custom-call(bf16[4,4,3,48,128]{4,3,2,1,0:T(8,128)(2,1)} %get-tuple-e, ...), custom_call_target="tpu_custom_call" | custom-call | tf_op jit(solution)/shard_map/pallas_call | solution.py:1096

commit v3 on v2

--- a/solution.py
+++ b/solution.py
@@ -225,7 +225,7 @@
                 score = score + score_col(p, head) * fields[p]
             score = score * scale
             weight = jnp.exp(score - jnp.max(score, axis=0, keepdims=True))
-            prob = weight / jnp.sum(weight, axis=0, keepdims=True)
+            prob = weight * (1.0 / jnp.sum(weight, axis=0, keepdims=True))
             probs[head, :, at] = prob
             both = matmul(value_map[head], mixture(prob, fields))
             part = slice(head * HDIM, (head + 1) * HDIM)
@@ -290,7 +290,7 @@
             totals = lax.fori_loop(low, high, blend, zero)
             for head in team:
                 part = slice(head * HDIM, (head + 1) * HDIM)
-                whole = mixed[head, :HDIM] / mixed[head, HDIM : HDIM + 1]
+                whole = mixed[head, :HDIM] * (1.0 / mixed[head, HDIM : HDIM + 1])
                 upper, rest = halves(whole)
                 attended[part, at] = upper
                 grad_out[part, at] = rest
@@ -1256,7 +1256,7 @@
     )
     cols_out[...] = columns.T
     for level in range(1, bits - 1):
-        for stream in (*trees, ones, twos):
+        for stream in (twos, ones, *trees):
             stream.advance(level)
     for tree in trees:
         tree.advance(bits - 1)

time: 164 us -> 163 us (level)
  no operation moved by 1% of the time
where the time goes in v3:
time: 163 us
  Pallas kernels  160 us (98%)
  local copies, waits for them, and re-layouts  2.36 us (1%)
    pallas_call x1, Pallas kernels, block_step(): pl.pallas_call(functools.partial(block_kernel, groups * count * length, g...  67 us
    pallas_call x1, Pallas kernels, reduce_all(): pl.pallas_call(functools.partial(reduce_kernel, count, groups), out_shape...  50.4 us
    pallas_call x1, Pallas kernels, gather_all(): pl.pallas_call(functools.partial(gather_kernel, count, groups), out_shape...  35.5 us
    pallas_call x1, Pallas kernels, update_all(): pl.pallas_call(functools.partial(update_kernel, groups), out_shape=tuple(...  6.93 us

profile of v3, /device:TPU:0, one launch (start us, length us, event | category | flops | bytes accessed | tf_op | source)
XLA Modules:
  0.0 163.1 jit_solution(4580685729754754206)
XLA Ops:
  0.7 1.4 copy.44
  2.0 1.0 copy.45.field_ref
  3.0 35.5 %shard_map.363 = (bf16[4,80,1024]{2,1,0:T(8,128)(2,1)}, f32[400,384]{1,0:T(8,128)}, f32[80,128]{1,0:T(8,128)}, f32[384,128]{1,0:T(8,128)}, bf16[4,8,48,384]{3,2,...) custom-call(s32[1,18]{1,0:T(1,128)} %bitcast.37, bf16[4,72,1024]{2,1,0:T(8,128)(2,1)} %copy.45.field_ref, ...), custom_call_target="tpu_custom_call" | custom-call | tf_op jit(solution)/shard_map/pallas_call | solution.py:1308
  38.6 67.0 %shard_map.364 = (bf16[1024,384]{1,0:T(8,128)(2,1)}, bf16[44,384,128]{2,1,0:T(8,128)(2,1)}, bf16[4,4,2,48,128]{4,3,2,1,0:T(8,128)(2,1)}, f32[16,384]{1,0:T(8,128)}, bf16[4,80,1024]{2,1,0:T(8,128)(2,1)}) custom-call(s32[1,1024]{1,0:T(1,128)} %bitcast.34, bf16[4,80,1024]{2,1,0:T(8,128)(2,1)} %get-tuple-element.60.fields_ref, ...), custom_call_target="tpu_custom_call" | custom-call | tf_op jit(solution)/shard_map/pallas_call | solution.py:592
  105.6 50.4 %shard_map.365 = (bf16[4,4,3,48,128]{4,3,2,1,0:T(8,128)(2,1)}, f32[8,48,128]{2,1,0:T(8,128)}, f32[48,2304]{1,0:T(8,128)}, f32[16,384]{1,0:T(8,128)}, bf16[4,80,1024]{2,1,0:T(8,128)(2,1)}) custom-call(bf16[44,4,2,48,128]{4,3,2,1,0:T(8,128)(2,1)} %bitcast.23, bf16[4,4,2,48,128]{4,3,2,1,0:T(8,128)(2,1)} %get-tuple-element.69.s_ref, ...), custom_call_target="tpu_custom_call" | custom-call | tf_op jit(solution)/shard_map/pallas_call | solution.py:985
  156.0 6.9 %shard_map.366 = (f32[5,18,384]{2,1,0:T(8,128)}, f32[5,18,384]{2,1,0:T(8,128)}, f32[5,18,384]{2,1,0:T(8,128)}, f32[5,18,384]{2,1,0:T(8,128)}, f32[4,48,384]{2,1,...) custom-call(bf16[4,4,3,48,128]{4,3,2,1,0:T(8,128)(2,1)} %get-tuple-e, ...), custom_call_target="tpu_custom_call" | custom-call | tf_op jit(solution)/shard_map/pallas_call | solution.py:1096
